TPU v7x, 256 devices: a whole 4x4x8 slice. The times are simulated.
256 devices in a mesh: fsdp: 64 (over x, z, core), rep: 4 (over y).
Axes of the slice: x: 4, y: 4, z: 8, core: 2. Of those that a mesh axis runs over, the one named last changes fastest.
Arguments:
- hidden_rows: bfloat16 [32768, 5120], P(('rep', 'fsdp')), parts along dimension 0, may hold values from -6 to 6
- queries: bfloat16 [32768, 4096], P(('rep', 'fsdp')), parts along dimension 0, may hold values from -6 to 6
- norm_gain: float32 [5120], replicated, may hold values from 0.1 to 1.9
- query_gain: float32 [128], replicated, may hold values from 0.5 to 12
- key_norm_gain: float32 [128], replicated, may hold values from 0.5 to 2
- key_matrix: bfloat16 [5120, 512], P('fsdp'), may hold values from -0.078125 to 0.078125
- value_matrix: bfloat16 [5120, 512], P('fsdp'), may hold values from -0.078125 to 0.078125
- lengths: int32 [256], P('rep'), parts along dimension 0, may hold values from 1 to 256, as said below
- owner: int32 [256], P('rep'), parts along dimension 0, may hold values from 0 to 63, as said below
Outputs:
- context: bfloat16 [32768, 4096], P(('rep', 'fsdp')), parts along dimension 0
There are 4 independent parts, one for each index of `rep`. A program takes and returns all parts, laid end to end along the dimension named above; an argument that names none is the same for every part. Nothing has to cross between parts.
Inputs may be any that keep to these rules, and one draw needn't show every extreme that they name: The lengths sum to 8192; one rollout has exactly 256 tokens. The rollouts of one owner hold at most 256 tokens together; some owner holds exactly 256.
All inputs are finite; a program needn't handle non-finite values.
Results may differ from a plain program's by a relative error of at most 0.012.
The roundings to bfloat16 on the way count: a program that leaves them out, or rounds other values in their place, can miss the bound.
Values may be sent and summed in bfloat16 or wider, within the bound.
No kernel may reach another device: no remote copies, remote signals or barrier semaphores. Data moves between devices by JAX's collectives and lax.ppermute only.
A program may use at most 128 MiB of HBM per device.

v0:
```python
import functools

import jax
import jax.numpy as jnp
import numpy as np
from jax import lax
from jax.experimental import pallas as pl
from jax.experimental.pallas import tpu as pltpu
from jax.sharding import Mesh, PartitionSpec as P

NX, NZ, NC = 4, 8, 2
NF = NX * NZ * NC
WIDTH = 5120
HEADS = 8
HEAD = 128
ROWS = 128
SHARD = WIDTH // NF
BLOCK = 8
HALO = 4
BLOCKS = ROWS // BLOCK
KTOK = NF * (BLOCK + HALO)
QTOK = NX * BLOCK
PAD = NX * HALO
X_ORDER = (0, -1, 1, 2)
Z_ORDER = (0, -1, 1, -2, 2, -3, 3, 4)
NEAR = 5

eps = 1e-06
rope_base = 1000000.0
BF = jnp.bfloat16
F32 = jnp.float32


def shift(value, axis, size, by):
    return lax.ppermute(value, axis, [(i, (i + by) % size) for i in range(size)])


def rollout_starts(lengths, owner, tokens):
    index = jnp.arange(lengths.shape[0], dtype=jnp.int32)
    earlier = (owner[None, :] < owner[:, None]) | (owner[None, :] == owner[:, None]) & (
        index[None, :] < index[:, None]
    )
    offset = jnp.sum(jnp.where(earlier, lengths[None, :], 0), axis=1)
    return jnp.max(jnp.where(offset[None, :] <= tokens[:, None], offset[None, :], 0), axis=1)


def rope_tables(positions):
    half = HEAD // 2
    steps = jnp.arange(half, dtype=F32) * (2.0 / HEAD)
    inverse = jnp.power(F32(rope_base), -steps)
    angles = positions.astype(F32)[:, None] * inverse[None, :]
    cosine = jnp.cos(angles)
    sine = jnp.sin(angles)
    return (
        jnp.concatenate([cosine, cosine], axis=1),
        jnp.concatenate([-sine, sine], axis=1),
    )


def normed_rope(value, gain, cosine, sine):
    mean_square = jnp.mean(value * value, axis=-1, keepdims=True)
    value = value * lax.rsqrt(mean_square + eps) * gain
    return value * cosine + pltpu.roll(value, HEAD // 2, 1) * sine


def pack_kernel(place, key, value, *out):
    for k, by in enumerate(X_ORDER):
        head = lax.rem(place[0] - by + NX, NX)
        lanes = pl.ds(pl.multiple_of(head * HEAD, HEAD), HEAD)
        out[k][:, :HEAD] = key[:, lanes]
        out[k][:, HEAD:] = value[:, lanes]


def stack_kernel(place, *refs):
    for k, by in enumerate(X_ORDER):
        refs[-1][lax.rem(place[0] + by + NX, NX)] = refs[k][...]


def norm_kernel(hidden, gain, out):
    block = 16

    def body(i, carry):
        rows = pl.ds(pl.multiple_of(i * block, block), block)
        value = hidden[rows, :].astype(F32)
        mean_square = jnp.mean(value * value, axis=-1, keepdims=True)
        value = value * lax.rsqrt(mean_square + eps) * gain[...]
        out[rows, :] = value.astype(BF)
        return carry

    lax.fori_loop(0, ROWS // block, body, 0)


def project(x, w, gain, cosine, sine):
    raw = jnp.dot(x, w, preferred_element_type=F32)
    return normed_rope(raw[:, :HEAD], gain, cosine, sine), raw[:, HEAD:]


def first_kernel(
    place,
    own,
    left,
    right,
    mine,
    mine2,
    other,
    other2,
    gain,
    cosine,
    sine,
    out,
    weight,
    tokens,
    sem,
    token_sem,
):
    z, c = place[1], place[2]
    copies = []
    for k, by in enumerate(Z_ORDER):
        at = lax.rem(z + by + NZ, NZ)
        near = k < NEAR
        for which, core in (((mine, mine2)[k >= NEAR], c), ((other, other2)[k >= NEAR], 1 - c)):
            copies.append(
                pltpu.make_async_copy(
                    which.at[k if near else k - NEAR], weight.at[:, at, core], sem.at[len(copies)]
                )
            )
    loads = []
    for k, chunk in enumerate((own, left, right)):
        loads.append(pltpu.make_async_copy(chunk, tokens.at[k], token_sem.at[k]))
    for copy in copies + loads:
        copy.start()
    for copy in copies:
        copy.wait()
    w = weight[...].reshape(WIDTH, 2 * HEAD)
    for load in loads:
        load.wait()

    def body(k, carry):
        rows = pl.ds(pl.multiple_of(k * ROWS, ROWS), ROWS)
        key, value = project(tokens[k], w, gain[...], cosine[rows, :], sine[rows, :])
        out[k, 0] = key
        out[k, 1] = value
        return carry

    lax.fori_loop(0, NX - 1, body, 0)


def second_kernel(far_a, far_b, weight, made, gain, cosine, sine, out, keep_k, keep_v):
    w = weight[...].reshape(WIDTH, 2 * HEAD)
    x = jnp.concatenate([far_a[...], far_b[...]], axis=0)
    rows = pl.ds((NX - 1) * ROWS, ROWS)
    far = project(x, w, gain[...], cosine[rows, :], sine[rows, :])
    for side, keep in enumerate((keep_k, keep_v)):
        for k in range(NX - 1):
            keep[pl.ds(k, ROWS, stride=NX), :] = made[k, side]
        keep[pl.ds(NX - 1, ROWS, stride=NX), :] = far[side]
        out[:, pl.ds(side * HEAD, HEAD)] = keep[...].astype(BF)


def split_kernel(place, q, *out):
    width = HEADS * HEAD
    for k, by in enumerate(X_ORDER):
        x = lax.rem(place[0] - by + NX, NX)
        out[k][...] = q[:, pl.ds(pl.multiple_of(x * width, width), width)]


def join_kernel(place, *refs):
    out = refs[-1]
    width = HEADS * HEAD
    for k, by in enumerate(X_ORDER):
        x = lax.rem(place[0] - by + NX, NX)
        out[:, pl.ds(pl.multiple_of(x * width, width), width)] = refs[k][...]


def prepare_kernel(q0, q1, q2, q3, gain, cosine, sine, out):
    def body(h, carry):
        lanes = pl.ds(pl.multiple_of(h * HEAD, HEAD), HEAD)
        done = []
        for k, q in enumerate((q0, q1, q2, q3)):
            rows = pl.ds(k * ROWS, ROWS)
            value = q[:, lanes].astype(F32)
            done.append(normed_rope(value, gain[...], cosine[rows, :], sine[rows, :]))
        for b in range(BLOCKS):
            rows = slice(b * BLOCK, (b + 1) * BLOCK)
            block = jnp.concatenate([value[rows] for value in done], axis=0)
            at = pl.ds(pl.multiple_of(h * QTOK, QTOK), QTOK)
            out[b, at, :] = block.astype(BF)
        return carry

    lax.fori_loop(0, HEADS, body, 0)


def attend_kernel(
    place,
    q_in,
    mine,
    mine2,
    mine3,
    other,
    other2,
    other3,
    token_in,
    start_in,
    key_token,
    o0,
    o1,
    o2,
    o3,
    kv,
    q,
    token,
    start,
    probs,
    scores,
    mixed,
    sem,
):
    copies = [
        pltpu.make_async_copy(q_in, q, sem.at[0]),
        pltpu.make_async_copy(token_in, token, sem.at[1]),
        pltpu.make_async_copy(start_in, start, sem.at[2]),
    ]
    for side, group in enumerate(((mine, mine2, mine3), (other, other2, other3))):
        at = 0
        for part in group:
            count = part.shape[0]
            copies.append(
                pltpu.make_async_copy(
                    part,
                    kv.at[side, pl.ds(at, count), pl.ds(PAD, NX * ROWS), :],
                    sem.at[len(copies)],
                )
            )
            at += count
    for copy in copies:
        copy.start()
    kv[:, :, :PAD, :] = jnp.zeros((NC, NZ, PAD, 2 * HEAD), BF)
    for copy in copies:
        copy.wait()
    scale = np.float32(1.0 / np.sqrt(HEAD))

    def window(b, side):
        rows = pl.ds(pl.multiple_of(b * QTOK, QTOK), PAD + QTOK)
        return kv[:, :, rows, pl.ds(side * HEAD, HEAD)].reshape(KTOK, HEAD)

    def score(b, slot):
        scores[slot] = lax.dot_general(
            q[b], window(b, 0), (((1,), (1,)), ((), ())), preferred_element_type=F32
        )

    score(0, 0)

    def body(i, carry):
        for slot in range(2):
            b = 2 * i + slot
            score(jnp.minimum(b + 1, BLOCKS - 1), 1 - slot)
            key = key_token[...] + b * BLOCK * NF
            seen = (key >= start[b]) & (key <= token[b])
            bias = jnp.where(seen, 0.0, -jnp.inf)
            for h in range(HEADS):
                head = pl.ds(h * QTOK, QTOK)
                s = scores[slot, head, :] * scale + bias
                weights = jnp.exp(s - jnp.max(s, axis=1, keepdims=True))
                total = jnp.sum(weights, axis=1, keepdims=True)
                probs[slot, head, :] = (weights * (1.0 / total)).astype(BF)
            m = jnp.dot(probs[slot], window(b, 1), preferred_element_type=F32)
            rows = pl.ds(pl.multiple_of(b * BLOCK, BLOCK), BLOCK)
            for h in range(HEADS):
                for k in range(NX):
                    at = h * QTOK + k * BLOCK
                    mixed[k, rows, pl.ds(h * HEAD, HEAD)] = m[at : at + BLOCK]
        return carry

    lax.fori_loop(0, BLOCKS // 2, body, 0)
    for k, out in enumerate((o0, o1, o2, o3)):
        out[...] = mixed[k].astype(BF)


def per_device(
    hidden_rows,
    queries,
    norm_gain,
    query_gain,
    key_norm_gain,
    key_matrix,
    value_matrix,
    lengths,
    owner,
):
    x, z, c = (lax.axis_index(a).astype(jnp.int32) for a in ("x", "z", "core"))
    zc = z * NC + c
    place = jnp.stack([x, z, c])
    vmem = pl.BlockSpec(memory_space=pltpu.VMEM)
    anywhere = pl.BlockSpec(memory_space=pl.ANY)
    smem = pl.BlockSpec(memory_space=pltpu.SMEM)
    rows = jnp.arange(ROWS, dtype=jnp.int32)
    chunk_x = jnp.stack([(x + by + NX) % NX for by in X_ORDER])
    token = rows[None, :] * NF + chunk_x[:, None] * (NZ * NC) + zc
    start = rollout_starts(lengths, owner, token.reshape(-1))
    key_cos, key_sin = rope_tables(token.reshape(-1) - start)

    def blocked(value):
        value = value.reshape(NX, BLOCKS, BLOCK).transpose(1, 0, 2)
        return value.reshape(BLOCKS, QTOK, 1)

    core = jnp.stack([c, 1 - c])
    around = jnp.stack([(z + by + NZ) % NZ for by in Z_ORDER])
    key_rows = jnp.arange(-HALO, BLOCK, dtype=jnp.int32)
    key_token = (
        key_rows[None, None, :, None] * NF
        + chunk_x[None, None, None, :] * (NZ * NC)
        + around[None, :, None, None] * NC
        + core[:, None, None, None]
    ).reshape(1, KTOK)

    seen_by = (blocked(token), blocked(start), key_token)

    bar = lax.optimization_barrier
    packed = pl.pallas_call(
        pack_kernel,
        in_specs=[smem, vmem, vmem],
        out_specs=[vmem] * NX,
        out_shape=[jax.ShapeDtypeStruct((SHARD, 2 * HEAD), BF)] * NX,
        name="pack_weights",
    )(place, key_matrix, value_matrix)
    hidden_rows, packed = bar((hidden_rows, packed))
    own = pl.pallas_call(
        norm_kernel,
        in_specs=[vmem, vmem],
        out_specs=vmem,
        out_shape=jax.ShapeDtypeStruct((ROWS, WIDTH), BF),
        name="norm_hidden",
    )(hidden_rows, norm_gain.reshape(1, WIDTH))
    piece = pl.pallas_call(
        stack_kernel,
        in_specs=[smem] + [vmem] * NX,
        out_specs=vmem,
        out_shape=jax.ShapeDtypeStruct((NX, SHARD, 2 * HEAD), BF),
        name="stack_weights",
    )(place, packed[0], *[shift(packed[k], "x", NX, -X_ORDER[k]) for k in range(1, NX)])

    parts = pl.pallas_call(
        split_kernel,
        in_specs=[smem, vmem],
        out_specs=[vmem] * NX,
        out_shape=[jax.ShapeDtypeStruct((ROWS, HEADS * HEAD), BF)] * NX,
        name="split_queries",
    )(place, queries)
    piece, own = bar((piece, own))
    left = shift(own, "x", NX, 1)
    right = shift(own, "x", NX, -1)

    cut = ROWS // 2
    pieces = [piece]
    up = down = piece
    for step in range(NZ // 2 - 1):
        up = shift(up, "z", NZ, 1)
        down = shift(down, "z", NZ, -1)
        if step == 0:
            up, down, seen_by, key_cos, key_sin, parts = bar(
                (up, down, seen_by, key_cos, key_sin, parts)
            )
        if step == 2:
            up, down, left, right = bar((up, down, left, right))
            far_a = shift(left[:cut], "x", NX, 1)
            far_b = shift(right[cut:], "x", NX, -1)
        pieces += [up, down]
    half = NX // 2
    last_a = shift(up[:half], "z", NZ, 1)
    last_b = shift(down[half:], "z", NZ, -1)
    pieces.append(jnp.concatenate([last_a, last_b], axis=0))
    mine, mine2 = jnp.stack(pieces[:NEAR]), jnp.stack(pieces[NEAR:])
    mine2, far_a, far_b = bar((mine2, far_a, far_b))
    other, other2 = shift(mine, "core", NC, 1), shift(mine2, "core", NC, 1)

    parts, far_a, far_b = bar((parts, far_a, far_b))
    got = [parts[0]] + [shift(parts[k], "x", NX, -X_ORDER[k]) for k in range(1, NX)]

    key_gain = key_norm_gain.reshape(1, HEAD)
    made_first, weight = pl.pallas_call(
        first_kernel,
        in_specs=[smem] + [anywhere] * 7 + [vmem] * 3,
        out_specs=[vmem] * 2,
        out_shape=[
            jax.ShapeDtypeStruct((NX - 1, 2, ROWS, HEAD), F32),
            jax.ShapeDtypeStruct((NX, NZ, NC, SHARD, 2 * HEAD), BF),
        ],
        scratch_shapes=[
            pltpu.VMEM((NX - 1, ROWS, WIDTH), BF),
            pltpu.SemaphoreType.DMA((2 * NZ,)),
            pltpu.SemaphoreType.DMA((NX - 1,)),
        ],
        compiler_params=pltpu.CompilerParams(vmem_limit_bytes=32 * 2**20),
        name="project_first",
    )(place, own, left, right, mine, mine2, other, other2, key_gain, key_cos, key_sin)
    made_kv = pl.pallas_call(
        second_kernel,
        in_specs=[vmem] * 7,
        out_specs=vmem,
        out_shape=jax.ShapeDtypeStruct((NX * ROWS, 2 * HEAD), BF),
        scratch_shapes=[pltpu.VMEM((NX * ROWS, HEAD), F32)] * 2,
        compiler_params=pltpu.CompilerParams(vmem_limit_bytes=32 * 2**20),
        name="project_last",
    )(far_a, far_b, weight, made_first, key_gain, key_cos, key_sin)
    def prepare(got):
        return pl.pallas_call(
            prepare_kernel,
            in_specs=[vmem] * 7,
            out_specs=vmem,
            out_shape=jax.ShapeDtypeStruct((BLOCKS, HEADS * QTOK, HEAD), BF),
            compiler_params=pltpu.CompilerParams(vmem_limit_bytes=32 * 2**20),
            name="prepare_queries",
        )(*got, query_gain.reshape(1, HEAD), key_cos, key_sin)

    up = down = made_kv
    first, second = [made_kv], []
    for step in range(NZ // 2 - 1):
        up = shift(up, "z", NZ, 1)
        down = shift(down, "z", NZ, -1)
        if step == 0:
            up, down, got = bar((up, down, got))
            ready = prepare(got)
        if step == 2:
            up, down, ready = bar((up, down, ready))
        (first if step < 2 else second).extend([up, down])
    half = NX * ROWS // 2
    third = jnp.concatenate(
        [shift(up[:half], "z", NZ, 1), shift(down[half:], "z", NZ, -1)], axis=0
    )
    groups = [jnp.stack(first), jnp.stack(second), third[None]]
    crossed = [shift(group, "core", NC, 1) for group in groups]

    mixed = pl.pallas_call(
        attend_kernel,
        in_specs=[smem] + [anywhere] * 9 + [vmem],
        out_specs=[vmem] * NX,
        out_shape=[jax.ShapeDtypeStruct((ROWS, HEADS * HEAD), BF)] * NX,
        scratch_shapes=[
            pltpu.VMEM((NC, NZ, PAD + NX * ROWS, 2 * HEAD), BF),
            pltpu.VMEM((BLOCKS, HEADS * QTOK, HEAD), BF),
            pltpu.VMEM((BLOCKS, QTOK, 1), jnp.int32),
            pltpu.VMEM((BLOCKS, QTOK, 1), jnp.int32),
            pltpu.VMEM((2, HEADS * QTOK, KTOK), BF),
            pltpu.VMEM((2, HEADS * QTOK, KTOK), F32),
            pltpu.VMEM((NX, ROWS, HEADS * HEAD), F32),
            pltpu.SemaphoreType.DMA((9,)),
        ],
        compiler_params=pltpu.CompilerParams(vmem_limit_bytes=40 * 2**20),
        name="attend",
    )(place, ready, *groups, *crossed, *seen_by)
    back = [mixed[0]] + [shift(mixed[k], "x", NX, X_ORDER[k]) for k in range(1, NX)]
    return pl.pallas_call(
        join_kernel,
        in_specs=[smem] + [vmem] * NX,
        out_specs=vmem,
        out_shape=jax.ShapeDtypeStruct((ROWS, NX * HEADS * HEAD), BF),
        name="join_heads",
    )(place, *back)


def solution(mesh):
    grid = Mesh(mesh.devices.reshape(NX, NZ, NC, mesh.devices.shape[1]), ("x", "z", "core", "rep"))
    fsdp = ("x", "z", "core")
    whole = P(("rep",) + fsdp, None)
    placed = (whole, whole, P(), P(), P(), P(fsdp, None), P(fsdp, None), P("rep"), P("rep"))
    return jax.shard_map(
        per_device, mesh=grid, in_specs=placed, out_specs=whole, check_vma=False
    )
```

profile of v0, /device:TPU:1, one launch (start us, length us, event | category | flops | bytes accessed | tf_op | source)
XLA Modules:
  0.0 145.3 jit_solution(2730193197166669300)
XLA Ops:
  0.0 0.7 pad_add_fusion.place
  0.7 1.6 %pack_weights.1 = (bf16[80,256]{1,0:T(8,128)(2,1)}, bf16[80,256]{1,0:T(8,128)(2,1)}, bf16[80,256]{1,0:T(8,128)(2,1)}, bf16[80,256]{1,0:T(8,128)(2,1)}) custom-call(s32[3]{0:T(128)} %pad_add_fusion.place, bf16[80,512]{1,0:T(8,128)(2,1)} %key.1, bf16[80,512]{1,0:T(8,128)(2,1)} %value.1), custom_call_target="tpu_custom_call" | custom-call | tf_op jit(solution)/shard_map/pack_weights/pallas_call | solution.py:319
  2.3 2.0 %collective-permute-start = (bf16[80,256]{1,0:T(8,128)(2,1)}, bf16[80,256]{1,0:T(8,128)(2,1)S(1)}, u32[]{:S(2)}, u32[]{:S(2)}) collective-permute-start(bf16[80,256]{1,0:T(8,128)(2,1)} %get-tuple-element.64), channel_id=1, source_target_pairs={{0,64},{64,128},{128,192},{192,0},{1,65},{65,129},{129,193},{193,1... | collective-permute-start | bytes 122888 | tf_op jit(solution)/shard_map/ppermute | solution.py:35
  4.3 1.3 collective-permute-start.1
  5.7 1.7 %collective-permute-start.2 = (bf16[80,256]{1,0:T(8,128)(2,1)}, bf16[80,256]{1,0:T(8,128)(2,1)S(1)}, u32[]{:S(2)}, u32[]{:S(2)}) collective-permute-start(bf16[80,256]{1,0:T(8,128)(2,1)} %get-tuple-element.66), channel_id=1, source_target_pairs={{0,128},{64,192},{128,0},{192,64},{1,129},{65,193},{129,1},{193,65... | collective-permute-start | bytes 122888 | tf_op jit(solution)/shard_map/ppermute | solution.py:35
  7.8 0.9 select_reduce_fusion.1
  9.1 3.7 %norm_hidden.1.own = bf16[128,5120]{1,0:T(8,128)(2,1)} custom-call(bf16[128,5120]{1,0:T(8,128)(2,1)} %hidden, f32[1,5120]{1,0:T(1,128)} %bitcast.64), custom_call_target="tpu_custom_call" | custom-call | tf_op jit(solution)/shard_map/norm_hidden/pallas_call | solution.py:327
  12.8 0.6 copy-done.11
  13.4 0.6 copy-done.13
  14.1 1.5 %stack_weights.1 = bf16[4,80,256]{2,1,0:T(8,128)(2,1)} custom-call(s32[3]{0:T(128)} %pad_add_fusion.place, bf16[80,256]{1,0:T(8,128)(2,1)} %get-tuple-element.63.refs_0_, bf16[80,256]{1,0:T(8,128)(2,1)} %copy-done.11, bf16[80,256]{1,0:T(8,128)(2,1)} %copy-done.12, bf16[80,256]{1,0:T(8,128)(2,1)} %copy-done.13), custom_call_target="tpu_custom_call" | custom-call | tf_op jit(solution)/shard_map/stack_weights/pallas_call | solution.py:334
  15.6 0.9 collective-permute-start.10
  16.5 0.6 collective-permute-start.9
  17.4 0.3 copy.13
  17.9 2.3 %split_queries.1 = (bf16[128,1024]{1,0:T(8,128)(2,1)}, bf16[128,1024]{1,0:T(8,128)(2,1)}, bf16[128,1024]{1,0:T(8,128)(2,1)}, bf16[128,1024]{1,0:T(8,128)(2,1)}) custom-call(s32[3]{0:T(128)} %pad_add_fusion.place, bf16[128,4096]{1,0:T(8,128)(2,1)} %q.1), custom_call_target="tpu_custom_call" | custom-call | tf_op jit(solution)/shard_map/split_queries/pallas_call | solution.py:342
  20.1 1.0 fusion
  21.1 0.2 pad_maximum_fusion.2
  21.4 1.7 %collective-permute-start.3 = (bf16[4,80,256]{2,1,0:T(8,128)(2,1)S(1)}, bf16[4,80,256]{2,1,0:T(8,128)(2,1)S(1)}, u32[]{:S(2)}, u32[]{:S(2)}) collective-permute-start(bf16[4,80,256]{2,1,0:T(8,128)(2,1)S(1)} %copy-done.7), channel_id=1, source_target_pairs={{0,8},{8,16},{16,24},{24,32},{32,40},{40,48},{48,56},{56,0},{1,9},... | collective-permute-start | bytes 491528 | tf_op jit(solution)/shard_map/ppermute | solution.py:35
  23.2 4.0 %collective-permute-start.4 = (bf16[4,80,256]{2,1,0:T(8,128)(2,1)S(1)}, bf16[4,80,256]{2,1,0:T(8,128)(2,1)S(1)}, u32[]{:S(2)}, u32[]{:S(2)}) collective-permute-start(bf16[4,80,256]{2,1,0:T(8,128)(2,1)S(1)} %copy-done.7), channel_id=1, source_target_pairs={{0,56},{8,0},{16,8},{24,16},{32,24},{40,32},{48,40},{56,48},{1,57}... | collective-permute-start | bytes 491528 | tf_op jit(solution)/shard_map/ppermute | solution.py:35
  27.2 2.9 %collective-permute-done.3 = bf16[4,80,256]{2,1,0:T(8,128)(2,1)S(1)} collective-permute-done((bf16[4,80,256]{2,1,0:T(8,128)(2,1)S(1)}, bf16[4,80,256]{2,1,0:T(8,128)(2,1)S(1)}, u32[]{:S(2)}, u32[]{:S(2)}) %collective-permute-start.3) | collective-permute-done | bytes 163872 | tf_op jit(solution)/shard_map/ppermute | solution.py:35
  30.1 2.8 %collective-permute-start.7 = (bf16[4,80,256]{2,1,0:T(8,128)(2,1)S(1)}, bf16[4,80,256]{2,1,0:T(8,128)(2,1)S(1)}, u32[]{:S(2)}, u32[]{:S(2)}) collective-permute-start(bf16[4,80,256]{2,1,0:T(8,128)(2,1)S(1)} %collective-permute-done.4), channel_id=1, source_target_pairs={{0,56},{8,0},{16,8},{24,16},{32,24},{40,32},{48,40},{56,48},{1,57}... | collective-permute-start | bytes 491528 | tf_op jit(solution)/shard_map/ppermute | solution.py:35
  32.9 3.0 %collective-permute-done.5 = bf16[4,80,256]{2,1,0:T(8,128)(2,1)S(1)} collective-permute-done((bf16[4,80,256]{2,1,0:T(8,128)(2,1)S(1)}, bf16[4,80,256]{2,1,0:T(8,128)(2,1)S(1)}, u32[]{:S(2)}, u32[]{:S(2)}) %collective-permute-start.5) | collective-permute-done | bytes 163872 | tf_op jit(solution)/shard_map/ppermute | solution.py:35
  35.9 2.7 %collective-permute-start.8 = (bf16[4,80,256]{2,1,0:T(8,128)(2,1)S(1)}, bf16[4,80,256]{2,1,0:T(8,128)(2,1)S(1)}, u32[]{:S(2)}, u32[]{:S(2)}) collective-permute-start(bf16[4,80,256]{2,1,0:T(8,128)(2,1)S(1)} %collective-permute-done.7), channel_id=1, source_target_pairs={{0,56},{8,0},{16,8},{24,16},{32,24},{40,32},{48,40},{56,48},{1,57}... | collective-permute-start | bytes 491528 | tf_op jit(solution)/shard_map/ppermute | solution.py:35
  38.6 3.0 %collective-permute-done.6 = bf16[4,80,256]{2,1,0:T(8,128)(2,1)S(1)} collective-permute-done((bf16[4,80,256]{2,1,0:T(8,128)(2,1)S(1)}, bf16[4,80,256]{2,1,0:T(8,128)(2,1)S(1)}, u32[]{:S(2)}, u32[]{:S(2)}) %collective-permute-start.6) | collective-permute-done | bytes 163872 | tf_op jit(solution)/shard_map/ppermute | solution.py:35
  41.5 3.0 %collective-permute-done.10.right = bf16[128,5120]{1,0:T(8,128)(2,1)S(1)} collective-permute-done((bf16[128,5120]{1,0:T(8,128)(2,1)}, bf16[128,5120]{1,0:T(8,128)(2,1)S(1)}, u32[]{:S(2)}, u32[]{:S(2)}) %collective-permute-start.10) | collective-permute-done | bytes 1310752 | tf_op jit(solution)/shard_map/ppermute | solution.py:35
  44.6 1.5 %collective-permute-done.9.left = bf16[128,5120]{1,0:T(8,128)(2,1)S(1)} collective-permute-done((bf16[128,5120]{1,0:T(8,128)(2,1)}, bf16[128,5120]{1,0:T(8,128)(2,1)S(1)}, u32[]{:S(2)}, u32[]{:S(2)}) %collective-permute-start.9) | collective-permute-done | bytes 1310752 | tf_op jit(solution)/shard_map/ppermute | solution.py:35
  46.3 2.9 %collective-permute-start.14 = (bf16[64,5120]{1,0:T(8,128)(2,1)S(1)}, bf16[64,5120]{1,0:T(8,128)(2,1)S(1)}, u32[]{:S(2)}, u32[]{:S(2)}) collective-permute-start(bf16[64,5120]{1,0:T(8,128)(2,1)S(1)} %slice.21), channel_id=1, source_target_pairs={{0,192},{64,0},{128,64},{192,128},{1,193},{65,1},{129,65},{193,129... | collective-permute-start | bytes 1966088 | tf_op jit(solution)/shard_map/ppermute | solution.py:35
  49.3 3.7 %collective-permute-start.15 = (bf16[5,4,80,256]{3,2,1,0:T(8,128)(2,1)S(1)}, bf16[5,4,80,256]{3,2,1,0:T(8,128)(2,1)S(1)}, u32[]{:S(2)}, u32[]{:S(2)}) collective-permute-start(bf16[5,4,80,256]{3,2,1,0:T(8,128)(2,1)S(1)} %bitcast_dynamic-update-slice_fusion.5.mine), channel_id=1, source_target_pairs={{0,4},{4,0},{1,5},{5,1},{2,6},{6,2},{3,7},{7,3},{8,12},{12,8},{9,1... | collective-permute-start | bytes 2457608 | tf_op jit(solution)/shard_map/ppermute | solution.py:35
  52.9 1.7 %collective-permute-start.11 = (bf16[2,80,256]{2,1,0:T(8,128)(2,1)S(1)}, bf16[2,80,256]{2,1,0:T(8,128)(2,1)S(1)}, u32[]{:S(2)}, u32[]{:S(2)}) collective-permute-start(bf16[2,80,256]{2,1,0:T(8,128)(2,1)S(1)} %slice.18), channel_id=1, source_target_pairs={{0,8},{8,16},{16,24},{24,32},{32,40},{40,48},{48,56},{56,0},{1,9},... | collective-permute-start | bytes 245768 | tf_op jit(solution)/shard_map/ppermute | solution.py:35
  54.6 4.0 %collective-permute-start.12 = (bf16[2,80,256]{2,1,0:T(8,128)(2,1)S(1)}, bf16[2,80,256]{2,1,0:T(8,128)(2,1)S(1)}, u32[]{:S(2)}, u32[]{:S(2)}) collective-permute-start(bf16[2,80,256]{2,1,0:T(8,128)(2,1)S(1)} %slice.19), channel_id=1, source_target_pairs={{0,56},{8,0},{16,8},{24,16},{32,24},{40,32},{48,40},{56,48},{1,57}... | collective-permute-start | bytes 245768 | tf_op jit(solution)/shard_map/ppermute | solution.py:35
  58.6 2.6 %collective-permute-done.11 = bf16[2,80,256]{2,1,0:T(8,128)(2,1)S(1)} collective-permute-done((bf16[2,80,256]{2,1,0:T(8,128)(2,1)S(1)}, bf16[2,80,256]{2,1,0:T(8,128)(2,1)S(1)}, u32[]{:S(2)}, u32[]{:S(2)}) %collective-permute-start.11) | collective-permute-done | bytes 81952 | tf_op jit(solution)/shard_map/ppermute | solution.py:35
  61.3 3.2 %collective-permute-start.16 = (bf16[3,4,80,256]{3,2,1,0:T(8,128)(2,1)S(1)}, bf16[3,4,80,256]{3,2,1,0:T(8,128)(2,1)S(1)}, u32[]{:S(2)}, u32[]{:S(2)}) collective-permute-start(bf16[3,4,80,256]{3,2,1,0:T(8,128)(2,1)S(1)} %pad_maximum_fusion.1.mine2), channel_id=1, source_target_pairs={{0,4},{4,0},{1,5},{5,1},{2,6},{6,2},{3,7},{7,3},{8,12},{12,8},{9,1... | collective-permute-start | bytes 1474568 | tf_op jit(solution)/shard_map/ppermute | solution.py:35
  64.5 3.1 %collective-permute-start.20 = (bf16[128,1024]{1,0:T(8,128)(2,1)S(1)}, bf16[128,1024]{1,0:T(8,128)(2,1)S(1)}, u32[]{:S(2)}, u32[]{:S(2)}) collective-permute-start(bf16[128,1024]{1,0:T(8,128)(2,1)S(1)} %copy-done.15), channel_id=1, source_target_pairs={{0,192},{64,0},{128,64},{192,128},{1,193},{65,1},{129,65},{193,129... | collective-permute-start | bytes 786440 | tf_op jit(solution)/shard_map/ppermute | solution.py:35
  67.7 1.2 collective-permute-start.21
  68.9 4.1 %project_first.1 = (f32[3,2,128,128]{3,2,1,0:T(8,128)S(1)}, bf16[4,8,2,80,256]{4,3,2,1,0:T(8,128)(2,1)S(1)}) custom-call(s32[3]{0:T(128)S(1)} %copy-done.4, bf16[128,5120]{1,0:T(8,128)(2,1)S(1)} %copy-done, bf16[128,5120]{1,0:T(8,128)(2,1)S(1)} %collective-permute-done.9.left, bf16[128,5120]{1,0:T(8,128)(2,1)S(1)} %collective-permute-done.10.right, ...), custom_call_target="tpu_custom_call" | custom-call | tf_op jit(solution)/shard_map/project_first/pallas_call | solution.py:380
  73.0 0.7 project_last.1
  73.7 2.0 %collective-permute-start.17 = (bf16[512,256]{1,0:T(8,128)(2,1)S(1)}, bf16[512,256]{1,0:T(8,128)(2,1)S(1)}, u32[]{:S(2)}, u32[]{:S(2)}) collective-permute-start(bf16[512,256]{1,0:T(8,128)(2,1)S(1)} %project_last.1), channel_id=1, source_target_pairs={{0,8},{8,16},{16,24},{24,32},{32,40},{40,48},{48,56},{56,0},{1,9},... | collective-permute-start | bytes 786440 | tf_op jit(solution)/shard_map/ppermute | solution.py:35
  75.7 4.0 %collective-permute-start.18 = (bf16[512,256]{1,0:T(8,128)(2,1)S(1)}, bf16[512,256]{1,0:T(8,128)(2,1)S(1)}, u32[]{:S(2)}, u32[]{:S(2)}) collective-permute-start(bf16[512,256]{1,0:T(8,128)(2,1)S(1)} %project_last.1), channel_id=1, source_target_pairs={{0,56},{8,0},{16,8},{24,16},{32,24},{40,32},{48,40},{56,48},{1,57}... | collective-permute-start | bytes 786440 | tf_op jit(solution)/shard_map/ppermute | solution.py:35
  79.8 1.0 collective-permute-done.21.q3
  80.8 5.0 %collective-permute-done.17 = bf16[512,256]{1,0:T(8,128)(2,1)S(1)} collective-permute-done((bf16[512,256]{1,0:T(8,128)(2,1)S(1)}, bf16[512,256]{1,0:T(8,128)(2,1)S(1)}, u32[]{:S(2)}, u32[]{:S(2)}) %collective-permute-start.17) | collective-permute-done | bytes 262176 | tf_op jit(solution)/shard_map/ppermute | solution.py:35
  85.8 2.7 %collective-permute-start.24 = (bf16[512,256]{1,0:T(8,128)(2,1)S(1)}, bf16[512,256]{1,0:T(8,128)(2,1)S(1)}, u32[]{:S(2)}, u32[]{:S(2)}) collective-permute-start(bf16[512,256]{1,0:T(8,128)(2,1)S(1)} %collective-permute-done.18), channel_id=1, source_target_pairs={{0,56},{8,0},{16,8},{24,16},{32,24},{40,32},{48,40},{56,48},{1,57}... | collective-permute-start | bytes 786440 | tf_op jit(solution)/shard_map/ppermute | solution.py:35
  88.6 5.2 %collective-permute-done.22 = bf16[512,256]{1,0:T(8,128)(2,1)S(1)} collective-permute-done((bf16[512,256]{1,0:T(8,128)(2,1)S(1)}, bf16[512,256]{1,0:T(8,128)(2,1)S(1)}, u32[]{:S(2)}, u32[]{:S(2)}) %collective-permute-start.22) | collective-permute-done | bytes 262176 | tf_op jit(solution)/shard_map/ppermute | solution.py:35
  93.8 2.1 %collective-permute-start.28 = (bf16[5,512,256]{2,1,0:T(8,128)(2,1)S(1)}, bf16[5,512,256]{2,1,0:T(8,128)(2,1)}, u32[]{:S(2)}, u32[]{:S(2)}) collective-permute-start(bf16[5,512,256]{2,1,0:T(8,128)(2,1)S(1)} %bitcast_dynamic-update-slice_fusion.mine), channel_id=1, source_target_pairs={{0,4},{4,0},{1,5},{5,1},{2,6},{6,2},{3,7},{7,3},{8,12},{12,8},{9,1... | collective-permute-start | bytes 3932168 | tf_op jit(solution)/shard_map/ppermute | solution.py:35
  95.9 1.5 %collective-permute-start.23 = (bf16[512,256]{1,0:T(8,128)(2,1)S(1)}, bf16[512,256]{1,0:T(8,128)(2,1)S(1)}, u32[]{:S(2)}, u32[]{:S(2)}) collective-permute-start(bf16[512,256]{1,0:T(8,128)(2,1)S(1)} %collective-permute-done.22), channel_id=1, source_target_pairs={{0,8},{8,16},{16,24},{24,32},{32,40},{40,48},{48,56},{56,0},{1,9},... | collective-permute-start | bytes 786440 | tf_op jit(solution)/shard_map/ppermute | solution.py:35
  97.5 1.2 collective-permute-start.25
  98.6 2.7 %prepare_queries.1.q_in = bf16[16,256,128]{2,1,0:T(8,128)(2,1)S(1)} custom-call(bf16[128,1024]{1,0:T(8,128)(2,1)S(1)} %copy-done.3, bf16[128,1024]{1,0:T(8,128)(2,1)S(1)} %collective-permute-done.19.q1, bf16[128,1024]{1,0:T(8,128)(2,1)S(1)} %collective-permute-done.20.q2, bf16[128,1024]{1,0:T(8,128)(2,1)S(1)} %collective-permute-done.21.q3, ...), custom_call_target="tpu_custom_call" | custom-call | tf_op jit(solution)/shard_map/prepare_queries/pallas_call | solution.py:406
  101.3 3.7 %collective-permute-done.23 = bf16[512,256]{1,0:T(8,128)(2,1)S(1)} collective-permute-done((bf16[512,256]{1,0:T(8,128)(2,1)S(1)}, bf16[512,256]{1,0:T(8,128)(2,1)S(1)}, u32[]{:S(2)}, u32[]{:S(2)}) %collective-permute-start.23) | collective-permute-done | bytes 262176 | tf_op jit(solution)/shard_map/ppermute | solution.py:35
  105.1 1.5 %collective-permute-start.29 = (bf16[2,512,256]{2,1,0:T(8,128)(2,1)S(1)}, bf16[2,512,256]{2,1,0:T(8,128)(2,1)}, u32[]{:S(2)}, u32[]{:S(2)}) collective-permute-start(bf16[2,512,256]{2,1,0:T(8,128)(2,1)S(1)} %pad_maximum_fusion.mine2), channel_id=1, source_target_pairs={{0,4},{4,0},{1,5},{5,1},{2,6},{6,2},{3,7},{7,3},{8,12},{12,8},{9,1... | collective-permute-start | bytes 1572872 | tf_op jit(solution)/shard_map/ppermute | solution.py:35
  106.6 1.6 %collective-permute-start.26 = (bf16[256,256]{1,0:T(8,128)(2,1)S(1)}, bf16[256,256]{1,0:T(8,128)(2,1)S(1)}, u32[]{:S(2)}, u32[]{:S(2)}) collective-permute-start(bf16[256,256]{1,0:T(8,128)(2,1)S(1)} %slice.22), channel_id=1, source_target_pairs={{0,8},{8,16},{16,24},{24,32},{32,40},{40,48},{48,56},{56,0},{1,9},... | collective-permute-start | bytes 393224 | tf_op jit(solution)/shard_map/ppermute | solution.py:35
  108.2 1.1 collective-permute-start.27
  109.3 3.6 %collective-permute-done.26 = bf16[256,256]{1,0:T(8,128)(2,1)S(1)} collective-permute-done((bf16[256,256]{1,0:T(8,128)(2,1)S(1)}, bf16[256,256]{1,0:T(8,128)(2,1)S(1)}, u32[]{:S(2)}, u32[]{:S(2)}) %collective-permute-start.26) | collective-permute-done | bytes 131104 | tf_op jit(solution)/shard_map/ppermute | solution.py:35
  113.0 1.2 collective-permute-start.30
  114.2 1.0 copy.15.start_in
  115.2 0.3 collective-permute-done.30.other3
  115.5 0.9 copy-done.1
  116.4 10.7 %attend.1 = (bf16[128,1024]{1,0:T(8,128)(2,1)S(1)}, bf16[128,1024]{1,0:T(8,128)(2,1)S(1)}, bf16[128,1024]{1,0:T(8,128)(2,1)S(1)}, bf16[128,1024]{1,0:T(8,128)(2,1)S(1)}) custom-call(s32[3]{0:T(128)S(1)} %copy-done.4, bf16[16,256,128]{2,1,0:T(8,128)(2,1)S(1)} %prepare_queries.1.q_in, bf16[5,512,256]{2,1,0:T(8,128)(2,1)S(1)} %bitcast_dynamic-update-slice_fusion.mine, ...), custom_call_target="tpu_custom_call" | custom-call | tf_op jit(solution)/shard_map/attend/pallas_call | solution.py:433
  127.1 0.7 copy-done.2
  127.8 0.2 collective-permute-start.31
  128.0 1.3 collective-permute-start.32
  129.3 1.8 %collective-permute-start.33 = (bf16[128,1024]{1,0:T(8,128)(2,1)S(1)}, bf16[128,1024]{1,0:T(8,128)(2,1)S(1)}, u32[]{:S(2)}, u32[]{:S(2)}) collective-permute-start(bf16[128,1024]{1,0:T(8,128)(2,1)S(1)} %get-tuple-element.112), channel_id=1, source_target_pairs={{0,128},{64,192},{128,0},{192,64},{1,129},{65,193},{129,1},{193,65... | collective-permute-start | bytes 786440 | tf_op jit(solution)/shard_map/ppermute | solution.py:35
  131.1 4.3 %collective-permute-done.31.refs_1_ = bf16[128,1024]{1,0:T(8,128)(2,1)S(1)} collective-permute-done((bf16[128,1024]{1,0:T(8,128)(2,1)S(1)}, bf16[128,1024]{1,0:T(8,128)(2,1)S(1)}, u32[]{:S(2)}, u32[]{:S(2)}) %collective-permute-start.31) | collective-permute-done | bytes 262176 | tf_op jit(solution)/shard_map/ppermute | solution.py:35
  135.4 1.1 collective-permute-done.32.refs_2_
  136.5 5.9 %collective-permute-done.33.refs_3_ = bf16[128,1024]{1,0:T(8,128)(2,1)S(1)} collective-permute-done((bf16[128,1024]{1,0:T(8,128)(2,1)S(1)}, bf16[128,1024]{1,0:T(8,128)(2,1)S(1)}, u32[]{:S(2)}, u32[]{:S(2)}) %collective-permute-start.33) | collective-permute-done | bytes 262176 | tf_op jit(solution)/shard_map/ppermute | solution.py:35
  142.4 0.7 copy-done.10
  143.1 2.2 %join_heads.1 = bf16[128,4096]{1,0:T(8,128)(2,1)} custom-call(s32[3]{0:T(128)} %pad_add_fusion.place, bf16[128,1024]{1,0:T(8,128)(2,1)} %copy-done.2, bf16[128,1024]{1,0:T(8,128)(2,1)} %copy-done.8, bf16[128,1024]{1,0:T(8,128)(2,1)} %copy-done.9, bf16[128,1024]{1,0:T(8,128)(2,1)} %copy-done.10), custom_call_target="tpu_custom_call" | custom-call | tf_op jit(solution)/shard_map/join_heads/pallas_call | solution.py:452
  (94 shorter events, 1.9 us)
Async XLA Ops:
  2.3 10.5 %collective-permute-start = (bf16[80,256]{1,0:T(8,128)(2,1)}, bf16[80,256]{1,0:T(8,128)(2,1)S(1)}, u32[]{:S(2)}, u32[]{:S(2)}) collective-permute-start(bf16[80,256]{1,0:T(8,128)(2,1)} %get-tuple-element.64), channel_id=1, source_target_pairs={{0,64},{64,128},{128,192},{192,0},{1,65},{65,129},{129,193},{193,1... | collective-permute-start | bytes 122888 | tf_op jit(solution)/shard_map/ppermute | solution.py:35
  4.3 8.5 %collective-permute-start.1 = (bf16[80,256]{1,0:T(8,128)(2,1)}, bf16[80,256]{1,0:T(8,128)(2,1)S(1)}, u32[]{:S(2)}, u32[]{:S(2)}) collective-permute-start(bf16[80,256]{1,0:T(8,128)(2,1)} %get-tuple-element.65), channel_id=1, source_target_pairs={{0,192},{64,0},{128,64},{192,128},{1,193},{65,1},{129,65},{193,129... | collective-permute-start | bytes 122888 | tf_op jit(solution)/shard_map/ppermute | solution.py:35
  5.7 7.2 %collective-permute-start.2 = (bf16[80,256]{1,0:T(8,128)(2,1)}, bf16[80,256]{1,0:T(8,128)(2,1)S(1)}, u32[]{:S(2)}, u32[]{:S(2)}) collective-permute-start(bf16[80,256]{1,0:T(8,128)(2,1)} %get-tuple-element.66), channel_id=1, source_target_pairs={{0,128},{64,192},{128,0},{192,64},{1,129},{65,193},{129,1},{193,65... | collective-permute-start | bytes 122888 | tf_op jit(solution)/shard_map/ppermute | solution.py:35
  12.8 0.6 copy-start.11
  12.8 0.6 copy-start.12
  13.4 0.6 copy-start.13
  15.6 29.0 %collective-permute-start.10 = (bf16[128,5120]{1,0:T(8,128)(2,1)}, bf16[128,5120]{1,0:T(8,128)(2,1)S(1)}, u32[]{:S(2)}, u32[]{:S(2)}) collective-permute-start(bf16[128,5120]{1,0:T(8,128)(2,1)} %norm_hidden.1.own), channel_id=1, source_target_pairs={{0,192},{64,0},{128,64},{192,128},{1,193},{65,1},{129,65},{193,129... | collective-permute-start | bytes 3932168 | tf_op jit(solution)/shard_map/ppermute | solution.py:35
  16.5 29.6 %collective-permute-start.9 = (bf16[128,5120]{1,0:T(8,128)(2,1)}, bf16[128,5120]{1,0:T(8,128)(2,1)S(1)}, u32[]{:S(2)}, u32[]{:S(2)}) collective-permute-start(bf16[128,5120]{1,0:T(8,128)(2,1)} %norm_hidden.1.own), channel_id=1, source_target_pairs={{0,64},{64,128},{128,192},{192,0},{1,65},{65,129},{129,193},{193,1... | collective-permute-start | bytes 3932168 | tf_op jit(solution)/shard_map/ppermute | solution.py:35
  20.1 1.3 copy-start.7
  21.4 8.7 %collective-permute-start.3 = (bf16[4,80,256]{2,1,0:T(8,128)(2,1)S(1)}, bf16[4,80,256]{2,1,0:T(8,128)(2,1)S(1)}, u32[]{:S(2)}, u32[]{:S(2)}) collective-permute-start(bf16[4,80,256]{2,1,0:T(8,128)(2,1)S(1)} %copy-done.7), channel_id=1, source_target_pairs={{0,8},{8,16},{16,24},{24,32},{32,40},{40,48},{48,56},{56,0},{1,9},... | collective-permute-start | bytes 491528 | tf_op jit(solution)/shard_map/ppermute | solution.py:35
  23.2 6.9 %collective-permute-start.4 = (bf16[4,80,256]{2,1,0:T(8,128)(2,1)S(1)}, bf16[4,80,256]{2,1,0:T(8,128)(2,1)S(1)}, u32[]{:S(2)}, u32[]{:S(2)}) collective-permute-start(bf16[4,80,256]{2,1,0:T(8,128)(2,1)S(1)} %copy-done.7), channel_id=1, source_target_pairs={{0,56},{8,0},{16,8},{24,16},{32,24},{40,32},{48,40},{56,48},{1,57}... | collective-permute-start | bytes 491528 | tf_op jit(solution)/shard_map/ppermute | solution.py:35
  30.1 5.8 %collective-permute-start.5 = (bf16[4,80,256]{2,1,0:T(8,128)(2,1)S(1)}, bf16[4,80,256]{2,1,0:T(8,128)(2,1)S(1)}, u32[]{:S(2)}, u32[]{:S(2)}) collective-permute-start(bf16[4,80,256]{2,1,0:T(8,128)(2,1)S(1)} %collective-permute-done.3), channel_id=1, source_target_pairs={{0,8},{8,16},{16,24},{24,32},{32,40},{40,48},{48,56},{56,0},{1,9},... | collective-permute-start | bytes 491528 | tf_op jit(solution)/shard_map/ppermute | solution.py:35
  30.1 5.8 %collective-permute-start.7 = (bf16[4,80,256]{2,1,0:T(8,128)(2,1)S(1)}, bf16[4,80,256]{2,1,0:T(8,128)(2,1)S(1)}, u32[]{:S(2)}, u32[]{:S(2)}) collective-permute-start(bf16[4,80,256]{2,1,0:T(8,128)(2,1)S(1)} %collective-permute-done.4), channel_id=1, source_target_pairs={{0,56},{8,0},{16,8},{24,16},{32,24},{40,32},{48,40},{56,48},{1,57}... | collective-permute-start | bytes 491528 | tf_op jit(solution)/shard_map/ppermute | solution.py:35
  35.9 5.7 %collective-permute-start.6 = (bf16[4,80,256]{2,1,0:T(8,128)(2,1)S(1)}, bf16[4,80,256]{2,1,0:T(8,128)(2,1)S(1)}, u32[]{:S(2)}, u32[]{:S(2)}) collective-permute-start(bf16[4,80,256]{2,1,0:T(8,128)(2,1)S(1)} %collective-permute-done.5), channel_id=1, source_target_pairs={{0,8},{8,16},{16,24},{24,32},{32,40},{40,48},{48,56},{56,0},{1,9},... | collective-permute-start | bytes 491528 | tf_op jit(solution)/shard_map/ppermute | solution.py:35
  35.9 5.7 %collective-permute-start.8 = (bf16[4,80,256]{2,1,0:T(8,128)(2,1)S(1)}, bf16[4,80,256]{2,1,0:T(8,128)(2,1)S(1)}, u32[]{:S(2)}, u32[]{:S(2)}) collective-permute-start(bf16[4,80,256]{2,1,0:T(8,128)(2,1)S(1)} %collective-permute-done.7), channel_id=1, source_target_pairs={{0,56},{8,0},{16,8},{24,16},{32,24},{40,32},{48,40},{56,48},{1,57}... | collective-permute-start | bytes 491528 | tf_op jit(solution)/shard_map/ppermute | solution.py:35
  46.1 15.2 %collective-permute-start.13 = (bf16[64,5120]{1,0:T(8,128)(2,1)S(1)}, bf16[64,5120]{1,0:T(8,128)(2,1)S(1)}, u32[]{:S(2)}, u32[]{:S(2)}) collective-permute-start(bf16[64,5120]{1,0:T(8,128)(2,1)S(1)} %slice.20), channel_id=1, source_target_pairs={{0,64},{64,128},{128,192},{192,0},{1,65},{65,129},{129,193},{193,1... | collective-permute-start | bytes 1966088 | tf_op jit(solution)/shard_map/ppermute | solution.py:35
  46.2 18.3 %copy-start.16 = (bf16[128,1024]{1,0:T(8,128)(2,1)S(1)}, bf16[128,1024]{1,0:T(8,128)(2,1)}, u32[]{:S(2)}) copy-start(bf16[128,1024]{1,0:T(8,128)(2,1)} %get-tuple-element.94) | copy-start | bytes 786436
  46.2 18.3 %copy-start.15 = (bf16[128,1024]{1,0:T(8,128)(2,1)S(1)}, bf16[128,1024]{1,0:T(8,128)(2,1)}, u32[]{:S(2)}) copy-start(bf16[128,1024]{1,0:T(8,128)(2,1)} %get-tuple-element.95) | copy-start | bytes 786436
  46.3 21.4 %copy-start.14 = (bf16[128,1024]{1,0:T(8,128)(2,1)S(1)}, bf16[128,1024]{1,0:T(8,128)(2,1)}, u32[]{:S(2)}) copy-start(bf16[128,1024]{1,0:T(8,128)(2,1)} %get-tuple-element.96) | copy-start | bytes 786436
  46.3 22.6 %copy-start = (bf16[128,5120]{1,0:T(8,128)(2,1)S(1)}, bf16[128,5120]{1,0:T(8,128)(2,1)}, u32[]{:S(2)}) copy-start(bf16[128,5120]{1,0:T(8,128)(2,1)} %norm_hidden.1.own) | copy-start | bytes 3932164
  46.3 22.6 %copy-start.4 = (s32[3]{0:T(128)S(1)}, s32[3]{0:T(128)}, u32[]{:S(2)}) copy-start(s32[3]{0:T(128)} %pad_add_fusion.place) | copy-start | bytes 40
  46.3 22.6 %copy-start.5 = (f32[128]{0:T(128)S(1)}, f32[128]{0:T(128)}, u32[]{:S(2)}) copy-start(f32[128]{0:T(128)} %param.13) | copy-start | bytes 1540
  46.3 15.0 %collective-permute-start.14 = (bf16[64,5120]{1,0:T(8,128)(2,1)S(1)}, bf16[64,5120]{1,0:T(8,128)(2,1)S(1)}, u32[]{:S(2)}, u32[]{:S(2)}) collective-permute-start(bf16[64,5120]{1,0:T(8,128)(2,1)S(1)} %slice.21), channel_id=1, source_target_pairs={{0,192},{64,0},{128,64},{192,128},{1,193},{65,1},{129,65},{193,129... | collective-permute-start | bytes 1966088 | tf_op jit(solution)/shard_map/ppermute | solution.py:35
  49.3 19.6 %collective-permute-start.15 = (bf16[5,4,80,256]{3,2,1,0:T(8,128)(2,1)S(1)}, bf16[5,4,80,256]{3,2,1,0:T(8,128)(2,1)S(1)}, u32[]{:S(2)}, u32[]{:S(2)}) collective-permute-start(bf16[5,4,80,256]{3,2,1,0:T(8,128)(2,1)S(1)} %bitcast_dynamic-update-slice_fusion.5.mine), channel_id=1, source_target_pairs={{0,4},{4,0},{1,5},{5,1},{2,6},{6,2},{3,7},{7,3},{8,12},{12,8},{9,1... | collective-permute-start | bytes 2457608 | tf_op jit(solution)/shard_map/ppermute | solution.py:35
  52.9 8.3 %collective-permute-start.11 = (bf16[2,80,256]{2,1,0:T(8,128)(2,1)S(1)}, bf16[2,80,256]{2,1,0:T(8,128)(2,1)S(1)}, u32[]{:S(2)}, u32[]{:S(2)}) collective-permute-start(bf16[2,80,256]{2,1,0:T(8,128)(2,1)S(1)} %slice.18), channel_id=1, source_target_pairs={{0,8},{8,16},{16,24},{24,32},{32,40},{40,48},{48,56},{56,0},{1,9},... | collective-permute-start | bytes 245768 | tf_op jit(solution)/shard_map/ppermute | solution.py:35
  54.6 6.6 %collective-permute-start.12 = (bf16[2,80,256]{2,1,0:T(8,128)(2,1)S(1)}, bf16[2,80,256]{2,1,0:T(8,128)(2,1)S(1)}, u32[]{:S(2)}, u32[]{:S(2)}) collective-permute-start(bf16[2,80,256]{2,1,0:T(8,128)(2,1)S(1)} %slice.19), channel_id=1, source_target_pairs={{0,56},{8,0},{16,8},{24,16},{32,24},{40,32},{48,40},{56,48},{1,57}... | collective-permute-start | bytes 245768 | tf_op jit(solution)/shard_map/ppermute | solution.py:35
  61.3 7.5 %collective-permute-start.16 = (bf16[3,4,80,256]{3,2,1,0:T(8,128)(2,1)S(1)}, bf16[3,4,80,256]{3,2,1,0:T(8,128)(2,1)S(1)}, u32[]{:S(2)}, u32[]{:S(2)}) collective-permute-start(bf16[3,4,80,256]{3,2,1,0:T(8,128)(2,1)S(1)} %pad_maximum_fusion.1.mine2), channel_id=1, source_target_pairs={{0,4},{4,0},{1,5},{5,1},{2,6},{6,2},{3,7},{7,3},{8,12},{12,8},{9,1... | collective-permute-start | bytes 1474568 | tf_op jit(solution)/shard_map/ppermute | solution.py:35
  64.5 15.3 %collective-permute-start.19 = (bf16[128,1024]{1,0:T(8,128)(2,1)S(1)}, bf16[128,1024]{1,0:T(8,128)(2,1)S(1)}, u32[]{:S(2)}, u32[]{:S(2)}) collective-permute-start(bf16[128,1024]{1,0:T(8,128)(2,1)S(1)} %copy-done.16), channel_id=1, source_target_pairs={{0,64},{64,128},{128,192},{192,0},{1,65},{65,129},{129,193},{193,1... | collective-permute-start | bytes 786440 | tf_op jit(solution)/shard_map/ppermute | solution.py:35
  64.5 15.3 %collective-permute-start.20 = (bf16[128,1024]{1,0:T(8,128)(2,1)S(1)}, bf16[128,1024]{1,0:T(8,128)(2,1)S(1)}, u32[]{:S(2)}, u32[]{:S(2)}) collective-permute-start(bf16[128,1024]{1,0:T(8,128)(2,1)S(1)} %copy-done.15), channel_id=1, source_target_pairs={{0,192},{64,0},{128,64},{192,128},{1,193},{65,1},{129,65},{193,129... | collective-permute-start | bytes 786440 | tf_op jit(solution)/shard_map/ppermute | solution.py:35
  67.7 13.2 %collective-permute-start.21 = (bf16[128,1024]{1,0:T(8,128)(2,1)S(1)}, bf16[128,1024]{1,0:T(8,128)(2,1)S(1)}, u32[]{:S(2)}, u32[]{:S(2)}) collective-permute-start(bf16[128,1024]{1,0:T(8,128)(2,1)S(1)} %copy-done.14), channel_id=1, source_target_pairs={{0,128},{64,192},{128,0},{192,64},{1,129},{65,193},{129,1},{193,65... | collective-permute-start | bytes 786440 | tf_op jit(solution)/shard_map/ppermute | solution.py:35
  73.7 24.9 %copy-start.3 = (bf16[128,1024]{1,0:T(8,128)(2,1)S(1)}, bf16[128,1024]{1,0:T(8,128)(2,1)}, u32[]{:S(2)}) copy-start(bf16[128,1024]{1,0:T(8,128)(2,1)} %get-tuple-element.99.q0) | copy-start | bytes 786436
  73.7 24.9 %copy-start.6 = (f32[128]{0:T(128)S(1)}, f32[128]{0:T(128)}, u32[]{:S(2)}) copy-start(f32[128]{0:T(128)} %param.12) | copy-start | bytes 1540
  73.7 12.1 %collective-permute-start.17 = (bf16[512,256]{1,0:T(8,128)(2,1)S(1)}, bf16[512,256]{1,0:T(8,128)(2,1)S(1)}, u32[]{:S(2)}, u32[]{:S(2)}) collective-permute-start(bf16[512,256]{1,0:T(8,128)(2,1)S(1)} %project_last.1), channel_id=1, source_target_pairs={{0,8},{8,16},{16,24},{24,32},{32,40},{40,48},{48,56},{56,0},{1,9},... | collective-permute-start | bytes 786440 | tf_op jit(solution)/shard_map/ppermute | solution.py:35
  75.7 10.1 %collective-permute-start.18 = (bf16[512,256]{1,0:T(8,128)(2,1)S(1)}, bf16[512,256]{1,0:T(8,128)(2,1)S(1)}, u32[]{:S(2)}, u32[]{:S(2)}) collective-permute-start(bf16[512,256]{1,0:T(8,128)(2,1)S(1)} %project_last.1), channel_id=1, source_target_pairs={{0,56},{8,0},{16,8},{24,16},{32,24},{40,32},{48,40},{56,48},{1,57}... | collective-permute-start | bytes 786440 | tf_op jit(solution)/shard_map/ppermute | solution.py:35
  85.8 7.9 %collective-permute-start.22 = (bf16[512,256]{1,0:T(8,128)(2,1)S(1)}, bf16[512,256]{1,0:T(8,128)(2,1)S(1)}, u32[]{:S(2)}, u32[]{:S(2)}) collective-permute-start(bf16[512,256]{1,0:T(8,128)(2,1)S(1)} %collective-permute-done.17), channel_id=1, source_target_pairs={{0,8},{8,16},{16,24},{24,32},{32,40},{40,48},{48,56},{56,0},{1,9},... | collective-permute-start | bytes 786440 | tf_op jit(solution)/shard_map/ppermute | solution.py:35
  85.8 7.9 %collective-permute-start.24 = (bf16[512,256]{1,0:T(8,128)(2,1)S(1)}, bf16[512,256]{1,0:T(8,128)(2,1)S(1)}, u32[]{:S(2)}, u32[]{:S(2)}) collective-permute-start(bf16[512,256]{1,0:T(8,128)(2,1)S(1)} %collective-permute-done.18), channel_id=1, source_target_pairs={{0,56},{8,0},{16,8},{24,16},{32,24},{40,32},{48,40},{56,48},{1,57}... | collective-permute-start | bytes 786440 | tf_op jit(solution)/shard_map/ppermute | solution.py:35
  93.8 21.7 %collective-permute-start.28 = (bf16[5,512,256]{2,1,0:T(8,128)(2,1)S(1)}, bf16[5,512,256]{2,1,0:T(8,128)(2,1)}, u32[]{:S(2)}, u32[]{:S(2)}) collective-permute-start(bf16[5,512,256]{2,1,0:T(8,128)(2,1)S(1)} %bitcast_dynamic-update-slice_fusion.mine), channel_id=1, source_target_pairs={{0,4},{4,0},{1,5},{5,1},{2,6},{6,2},{3,7},{7,3},{8,12},{12,8},{9,1... | collective-permute-start | bytes 3932168 | tf_op jit(solution)/shard_map/ppermute | solution.py:35
  95.9 9.1 %collective-permute-start.23 = (bf16[512,256]{1,0:T(8,128)(2,1)S(1)}, bf16[512,256]{1,0:T(8,128)(2,1)S(1)}, u32[]{:S(2)}, u32[]{:S(2)}) collective-permute-start(bf16[512,256]{1,0:T(8,128)(2,1)S(1)} %collective-permute-done.22), channel_id=1, source_target_pairs={{0,8},{8,16},{16,24},{24,32},{32,40},{40,48},{48,56},{56,0},{1,9},... | collective-permute-start | bytes 786440 | tf_op jit(solution)/shard_map/ppermute | solution.py:35
  97.5 7.5 %collective-permute-start.25 = (bf16[512,256]{1,0:T(8,128)(2,1)S(1)}, bf16[512,256]{1,0:T(8,128)(2,1)S(1)}, u32[]{:S(2)}, u32[]{:S(2)}) collective-permute-start(bf16[512,256]{1,0:T(8,128)(2,1)S(1)} %collective-permute-done.24), channel_id=1, source_target_pairs={{0,56},{8,0},{16,8},{24,16},{32,24},{40,32},{48,40},{56,48},{1,57}... | collective-permute-start | bytes 786440 | tf_op jit(solution)/shard_map/ppermute | solution.py:35
  105.1 10.4 %collective-permute-start.29 = (bf16[2,512,256]{2,1,0:T(8,128)(2,1)S(1)}, bf16[2,512,256]{2,1,0:T(8,128)(2,1)}, u32[]{:S(2)}, u32[]{:S(2)}) collective-permute-start(bf16[2,512,256]{2,1,0:T(8,128)(2,1)S(1)} %pad_maximum_fusion.mine2), channel_id=1, source_target_pairs={{0,4},{4,0},{1,5},{5,1},{2,6},{6,2},{3,7},{7,3},{8,12},{12,8},{9,1... | collective-permute-start | bytes 1572872 | tf_op jit(solution)/shard_map/ppermute | solution.py:35
  106.6 6.4 %collective-permute-start.26 = (bf16[256,256]{1,0:T(8,128)(2,1)S(1)}, bf16[256,256]{1,0:T(8,128)(2,1)S(1)}, u32[]{:S(2)}, u32[]{:S(2)}) collective-permute-start(bf16[256,256]{1,0:T(8,128)(2,1)S(1)} %slice.22), channel_id=1, source_target_pairs={{0,8},{8,16},{16,24},{24,32},{32,40},{40,48},{48,56},{56,0},{1,9},... | collective-permute-start | bytes 393224 | tf_op jit(solution)/shard_map/ppermute | solution.py:35
  108.2 4.8 %collective-permute-start.27 = (bf16[256,256]{1,0:T(8,128)(2,1)S(1)}, bf16[256,256]{1,0:T(8,128)(2,1)S(1)}, u32[]{:S(2)}, u32[]{:S(2)}) collective-permute-start(bf16[256,256]{1,0:T(8,128)(2,1)S(1)} %slice.23), channel_id=1, source_target_pairs={{0,56},{8,0},{16,8},{24,16},{32,24},{40,32},{48,40},{56,48},{1,57}... | collective-permute-start | bytes 393224 | tf_op jit(solution)/shard_map/ppermute | solution.py:35
  113.0 2.5 %collective-permute-start.30 = (bf16[1,512,256]{2,1,0:T(8,128)(2,1)S(1)}, bf16[1,512,256]{2,1,0:T(8,128)(2,1)}, u32[]{:S(2)}, u32[]{:S(2)}) collective-permute-start(bf16[1,512,256]{2,1,0:T(8,128)(2,1)S(1)} %maximum_bitcast_fusion.mine3), channel_id=1, source_target_pairs={{0,4},{4,0},{1,5},{5,1},{2,6},{6,2},{3,7},{7,3},{8,12},{12,8},{9,1... | collective-permute-start | bytes 786440 | tf_op jit(solution)/shard_map/ppermute | solution.py:35
  115.5 1.0 copy-start.1
  127.1 0.7 copy-start.2
  127.8 7.5 %collective-permute-start.31 = (bf16[128,1024]{1,0:T(8,128)(2,1)S(1)}, bf16[128,1024]{1,0:T(8,128)(2,1)S(1)}, u32[]{:S(2)}, u32[]{:S(2)}) collective-permute-start(bf16[128,1024]{1,0:T(8,128)(2,1)S(1)} %get-tuple-element.110), channel_id=1, source_target_pairs={{0,192},{64,0},{128,64},{192,128},{1,193},{65,1},{129,65},{193,129... | collective-permute-start | bytes 786440 | tf_op jit(solution)/shard_map/ppermute | solution.py:35
  128.0 8.4 %collective-permute-start.32 = (bf16[128,1024]{1,0:T(8,128)(2,1)S(1)}, bf16[128,1024]{1,0:T(8,128)(2,1)S(1)}, u32[]{:S(2)}, u32[]{:S(2)}) collective-permute-start(bf16[128,1024]{1,0:T(8,128)(2,1)S(1)} %get-tuple-element.111), channel_id=1, source_target_pairs={{0,64},{64,128},{128,192},{192,0},{1,65},{65,129},{129,193},{193,1... | collective-permute-start | bytes 786440 | tf_op jit(solution)/shard_map/ppermute | solution.py:35
  129.3 13.1 %collective-permute-start.33 = (bf16[128,1024]{1,0:T(8,128)(2,1)S(1)}, bf16[128,1024]{1,0:T(8,128)(2,1)S(1)}, u32[]{:S(2)}, u32[]{:S(2)}) collective-permute-start(bf16[128,1024]{1,0:T(8,128)(2,1)S(1)} %get-tuple-element.112), channel_id=1, source_target_pairs={{0,128},{64,192},{128,0},{192,64},{1,129},{65,193},{129,1},{193,65... | collective-permute-start | bytes 786440 | tf_op jit(solution)/shard_map/ppermute | solution.py:35
  135.4 7.0 %copy-start.8 = (bf16[128,1024]{1,0:T(8,128)(2,1)}, bf16[128,1024]{1,0:T(8,128)(2,1)S(1)}, u32[]{:S(2)}) copy-start(bf16[128,1024]{1,0:T(8,128)(2,1)S(1)} %collective-permute-done.31.refs_1_) | copy-start | bytes 786436
  136.5 5.9 %copy-start.9 = (bf16[128,1024]{1,0:T(8,128)(2,1)}, bf16[128,1024]{1,0:T(8,128)(2,1)S(1)}, u32[]{:S(2)}) copy-start(bf16[128,1024]{1,0:T(8,128)(2,1)S(1)} %collective-permute-done.32.refs_2_) | copy-start | bytes 786436
  142.4 0.7 copy-start.10
where the time goes:
time: 146 us; the launch traced here: 145 us
  starting transfers between devices  59.7 us (41%)
  waiting for transfers between devices  46.2 us (32%)
  Pallas kernels  29.5 us (20%)
  local copies, waits for them, and re-layouts  5.74 us (4%)
  other arithmetic  3.67 us (3%)
    ppermute x34, starting transfers between devices, shift(): lax.ppermute(value, axis, [(i, (i + by) % size) for i in range(size)])  59.7 us
    ppermute x34, waiting for transfers between devices, shift(): lax.ppermute(value, axis, [(i, (i + by) % size) for i in range(size)])  46.2 us
    pallas_call x1, Pallas kernels, per_device(): pl.pallas_call(attend_kernel, in_specs=[smem] + [anywhere] * 9 + [vmem],...  10.7 us
    pallas_call x1, Pallas kernels, per_device(): pl.pallas_call(first_kernel, in_specs=[smem] + [anywhere] * 7 + [vmem] *...  4.08 us
    pallas_call x1, Pallas kernels, per_device(): pl.pallas_call(norm_kernel, in_specs=[vmem, vmem], out_specs=vmem, out_sh...  3.73 us
    unnamed x42, local copies, waits for them, and re-layouts  3.72 us
  transfers between devices with their start and end apart: 34, of which 15 were waited for; matrix products, arithmetic and copies ran while one was open for 4% of the time, Pallas kernels for 9%

commit v1 on v0

--- a/solution.py
+++ b/solution.py
@@ -251,11 +251,11 @@
     score(0, 0)
 
     def body(i, carry):
-        for slot in range(2):
-            b = 2 * i + slot
+        for j in range(4):
+            b, slot = 4 * i + j, j % 2
             score(jnp.minimum(b + 1, BLOCKS - 1), 1 - slot)
             key = key_token[...] + b * BLOCK * NF
-            seen = (key >= start[b]) & (key <= token[b])
+            seen = (key >= start[b, :, :1]) & (key <= token[b, :, :1])
             bias = jnp.where(seen, 0.0, -jnp.inf)
             for h in range(HEADS):
                 head = pl.ds(h * QTOK, QTOK)
@@ -271,7 +271,7 @@
                     mixed[k, rows, pl.ds(h * HEAD, HEAD)] = m[at : at + BLOCK]
         return carry
 
-    lax.fori_loop(0, BLOCKS // 2, body, 0)
+    lax.fori_loop(0, BLOCKS // 4, body, 0)
     for k, out in enumerate((o0, o1, o2, o3)):
         out[...] = mixed[k].astype(BF)
 
@@ -301,7 +301,7 @@
 
     def blocked(value):
         value = value.reshape(NX, BLOCKS, BLOCK).transpose(1, 0, 2)
-        return value.reshape(BLOCKS, QTOK, 1)
+        return jnp.broadcast_to(value.reshape(BLOCKS, QTOK, 1), (BLOCKS, QTOK, HEAD))
 
     core = jnp.stack([c, 1 - c])
     around = jnp.stack([(z + by + NZ) % NZ for by in Z_ORDER])
@@ -420,8 +420,6 @@
         if step == 0:
             up, down, got = bar((up, down, got))
             ready = prepare(got)
-        if step == 2:
-            up, down, ready = bar((up, down, ready))
         (first if step < 2 else second).extend([up, down])
     half = NX * ROWS // 2
     third = jnp.concatenate(
@@ -438,8 +436,8 @@
         scratch_shapes=[
             pltpu.VMEM((NC, NZ, PAD + NX * ROWS, 2 * HEAD), BF),
             pltpu.VMEM((BLOCKS, HEADS * QTOK, HEAD), BF),
-            pltpu.VMEM((BLOCKS, QTOK, 1), jnp.int32),
-            pltpu.VMEM((BLOCKS, QTOK, 1), jnp.int32),
+            pltpu.VMEM((BLOCKS, QTOK, HEAD), jnp.int32),
+            pltpu.VMEM((BLOCKS, QTOK, HEAD), jnp.int32),
             pltpu.VMEM((2, HEADS * QTOK, KTOK), BF),
             pltpu.VMEM((2, HEADS * QTOK, KTOK), F32),
             pltpu.VMEM((NX, ROWS, HEADS * HEAD), F32),

time: 146 us -> 145 us (level)
  waiting for transfers between devices: 46.2 us -> 52.9 us
  starting transfers between devices: 59.7 us -> 57 us
  Pallas kernels: 29.5 us -> 27.3 us
  local copies, waits for them, and re-layouts: 5.74 us -> 3.84 us
    ppermute x34, waiting for transfers between devices: 46.2 us -> 52.9 us  [shift(): lax.ppermute(value, axis, [(i, (i + by) % size) for i in range(size)])]
    ppermute x34, starting transfers between devices: 59.7 us -> 57 us  [shift(): lax.ppermute(value, axis, [(i, (i + by) % size) for i in range(size)])]
    pallas_call x1, Pallas kernels: 10.7 us -> 8.44 us  [per_device(): pl.pallas_call(attend_kernel, in_specs=[smem] + [anywhere] * 9 + [vmem],...]
    unnamed x42 -> x40, local copies, waits for them, and re-layouts: 3.72 us -> 2.78 us
  transfers between devices with their start and end apart: 34 -> 34, of which waited for: 15 -> 17; matrix products, arithmetic and copies ran while one was open for 4% -> 3% of each run, Pallas kernels for 9% -> 9%
where the time goes in v1:
time: 145 us
  starting transfers between devices  57 us (39%)
  waiting for transfers between devices  52.9 us (36%)
  Pallas kernels  27.3 us (19%)
  local copies, waits for them, and re-layouts  3.84 us (3%)
  other arithmetic  3.64 us (3%)
    ppermute x34, starting transfers between devices, shift(): lax.ppermute(value, axis, [(i, (i + by) % size) for i in range(size)])  57 us
    ppermute x34, waiting for transfers between devices, shift(): lax.ppermute(value, axis, [(i, (i + by) % size) for i in range(size)])  52.9 us
    pallas_call x1, Pallas kernels, per_device(): pl.pallas_call(attend_kernel, in_specs=[smem] + [anywhere] * 9 + [vmem],...  8.44 us
    pallas_call x1, Pallas kernels, per_device(): pl.pallas_call(first_kernel, in_specs=[smem] + [anywhere] * 7 + [vmem] *...  4.09 us
    pallas_call x1, Pallas kernels, per_device(): pl.pallas_call(norm_kernel, in_specs=[vmem, vmem], out_specs=vmem, out_sh...  3.74 us
  transfers between devices with their start and end apart: 34, of which 17 were waited for; matrix products, arithmetic and copies ran while one was open for 3% of the time, Pallas kernels for 9%

profile of v1, /device:TPU:1, one launch (start us, length us, event | category | flops | bytes accessed | tf_op | source)
XLA Modules:
  0.0 145.1 jit_solution(1377808342431721130)
XLA Ops:
  0.0 0.7 pad_add_fusion.place
  0.7 1.6 %pack_weights.1 = (bf16[80,256]{1,0:T(8,128)(2,1)}, bf16[80,256]{1,0:T(8,128)(2,1)}, bf16[80,256]{1,0:T(8,128)(2,1)}, bf16[80,256]{1,0:T(8,128)(2,1)}) custom-call(s32[3]{0:T(128)} %pad_add_fusion.place, bf16[80,512]{1,0:T(8,128)(2,1)} %key.1, bf16[80,512]{1,0:T(8,128)(2,1)} %value.1), custom_call_target="tpu_custom_call" | custom-call | tf_op jit(solution)/shard_map/pack_weights/pallas_call | solution.py:319
  2.3 2.0 %collective-permute-start = (bf16[80,256]{1,0:T(8,128)(2,1)}, bf16[80,256]{1,0:T(8,128)(2,1)S(1)}, u32[]{:S(2)}, u32[]{:S(2)}) collective-permute-start(bf16[80,256]{1,0:T(8,128)(2,1)} %get-tuple-element.61), channel_id=1, source_target_pairs={{0,64},{64,128},{128,192},{192,0},{1,65},{65,129},{129,193},{193,1... | collective-permute-start | bytes 122888 | tf_op jit(solution)/shard_map/ppermute | solution.py:35
  4.3 1.3 collective-permute-start.1
  5.7 1.7 %collective-permute-start.2 = (bf16[80,256]{1,0:T(8,128)(2,1)}, bf16[80,256]{1,0:T(8,128)(2,1)S(1)}, u32[]{:S(2)}, u32[]{:S(2)}) collective-permute-start(bf16[80,256]{1,0:T(8,128)(2,1)} %get-tuple-element.63), channel_id=1, source_target_pairs={{0,128},{64,192},{128,0},{192,64},{1,129},{65,193},{129,1},{193,65... | collective-permute-start | bytes 122888 | tf_op jit(solution)/shard_map/ppermute | solution.py:35
  7.8 0.9 select_reduce_fusion.1
  9.1 0.1 select_reduce_fusion
  9.2 3.7 %norm_hidden.1.own = bf16[128,5120]{1,0:T(8,128)(2,1)} custom-call(bf16[128,5120]{1,0:T(8,128)(2,1)} %hidden, f32[1,5120]{1,0:T(1,128)} %bitcast.66), custom_call_target="tpu_custom_call" | custom-call | tf_op jit(solution)/shard_map/norm_hidden/pallas_call | solution.py:327
  12.9 0.6 copy-done.10
  13.6 0.6 copy-done.12
  14.2 1.5 %stack_weights.1 = bf16[4,80,256]{2,1,0:T(8,128)(2,1)} custom-call(s32[3]{0:T(128)} %pad_add_fusion.place, bf16[80,256]{1,0:T(8,128)(2,1)} %get-tuple-element.60.refs_0_, bf16[80,256]{1,0:T(8,128)(2,1)} %copy-done.10, bf16[80,256]{1,0:T(8,128)(2,1)} %copy-done.11, bf16[80,256]{1,0:T(8,128)(2,1)} %copy-done.12), custom_call_target="tpu_custom_call" | custom-call | tf_op jit(solution)/shard_map/stack_weights/pallas_call | solution.py:334
  15.7 0.9 collective-permute-start.10
  16.6 0.6 collective-permute-start.9
  17.2 0.1 reshape.278
  17.5 0.1 add.283.key_token
  17.6 2.3 %split_queries.1 = (bf16[128,1024]{1,0:T(8,128)(2,1)}, bf16[128,1024]{1,0:T(8,128)(2,1)}, bf16[128,1024]{1,0:T(8,128)(2,1)}, bf16[128,1024]{1,0:T(8,128)(2,1)}) custom-call(s32[3]{0:T(128)} %pad_add_fusion.place, bf16[128,4096]{1,0:T(8,128)(2,1)} %q.1), custom_call_target="tpu_custom_call" | custom-call | tf_op jit(solution)/shard_map/split_queries/pallas_call | solution.py:342
  20.0 1.0 fusion
  21.0 0.2 pad_maximum_fusion.2
  21.2 5.7 %collective-permute-start.4 = (bf16[4,80,256]{2,1,0:T(8,128)(2,1)S(1)}, bf16[4,80,256]{2,1,0:T(8,128)(2,1)S(1)}, u32[]{:S(2)}, u32[]{:S(2)}) collective-permute-start(bf16[4,80,256]{2,1,0:T(8,128)(2,1)S(1)} %copy-done.6), channel_id=1, source_target_pairs={{0,56},{8,0},{16,8},{24,16},{32,24},{40,32},{48,40},{56,48},{1,57}... | collective-permute-start | bytes 491528 | tf_op jit(solution)/shard_map/ppermute | solution.py:35
  26.9 2.2 %collective-permute-done.4 = bf16[4,80,256]{2,1,0:T(8,128)(2,1)S(1)} collective-permute-done((bf16[4,80,256]{2,1,0:T(8,128)(2,1)S(1)}, bf16[4,80,256]{2,1,0:T(8,128)(2,1)S(1)}, u32[]{:S(2)}, u32[]{:S(2)}) %collective-permute-start.4) | collective-permute-done | bytes 163872 | tf_op jit(solution)/shard_map/ppermute | solution.py:35
  29.1 3.4 %collective-permute-done.3 = bf16[4,80,256]{2,1,0:T(8,128)(2,1)S(1)} collective-permute-done((bf16[4,80,256]{2,1,0:T(8,128)(2,1)S(1)}, bf16[4,80,256]{2,1,0:T(8,128)(2,1)S(1)}, u32[]{:S(2)}, u32[]{:S(2)}) %collective-permute-start.3) | collective-permute-done | bytes 163872 | tf_op jit(solution)/shard_map/ppermute | solution.py:35
  32.5 0.1 broadcast_in_dim.35.start_in
  32.6 0.1 broadcast_in_dim.30.token_in
  32.9 2.7 %collective-permute-start.7 = (bf16[4,80,256]{2,1,0:T(8,128)(2,1)S(1)}, bf16[4,80,256]{2,1,0:T(8,128)(2,1)S(1)}, u32[]{:S(2)}, u32[]{:S(2)}) collective-permute-start(bf16[4,80,256]{2,1,0:T(8,128)(2,1)S(1)} %collective-permute-done.4), channel_id=1, source_target_pairs={{0,56},{8,0},{16,8},{24,16},{32,24},{40,32},{48,40},{56,48},{1,57}... | collective-permute-start | bytes 491528 | tf_op jit(solution)/shard_map/ppermute | solution.py:35
  35.5 3.0 %collective-permute-done.5 = bf16[4,80,256]{2,1,0:T(8,128)(2,1)S(1)} collective-permute-done((bf16[4,80,256]{2,1,0:T(8,128)(2,1)S(1)}, bf16[4,80,256]{2,1,0:T(8,128)(2,1)S(1)}, u32[]{:S(2)}, u32[]{:S(2)}) %collective-permute-start.5) | collective-permute-done | bytes 163872 | tf_op jit(solution)/shard_map/ppermute | solution.py:35
  38.5 2.7 %collective-permute-start.8 = (bf16[4,80,256]{2,1,0:T(8,128)(2,1)S(1)}, bf16[4,80,256]{2,1,0:T(8,128)(2,1)S(1)}, u32[]{:S(2)}, u32[]{:S(2)}) collective-permute-start(bf16[4,80,256]{2,1,0:T(8,128)(2,1)S(1)} %collective-permute-done.7), channel_id=1, source_target_pairs={{0,56},{8,0},{16,8},{24,16},{32,24},{40,32},{48,40},{56,48},{1,57}... | collective-permute-start | bytes 491528 | tf_op jit(solution)/shard_map/ppermute | solution.py:35
  41.2 3.0 %collective-permute-done.6 = bf16[4,80,256]{2,1,0:T(8,128)(2,1)S(1)} collective-permute-done((bf16[4,80,256]{2,1,0:T(8,128)(2,1)S(1)}, bf16[4,80,256]{2,1,0:T(8,128)(2,1)S(1)}, u32[]{:S(2)}, u32[]{:S(2)}) %collective-permute-start.6) | collective-permute-done | bytes 163872 | tf_op jit(solution)/shard_map/ppermute | solution.py:35
  44.2 0.5 collective-permute-done.10.right
  44.7 1.5 %collective-permute-done.9.left = bf16[128,5120]{1,0:T(8,128)(2,1)S(1)} collective-permute-done((bf16[128,5120]{1,0:T(8,128)(2,1)}, bf16[128,5120]{1,0:T(8,128)(2,1)S(1)}, u32[]{:S(2)}, u32[]{:S(2)}) %collective-permute-start.9) | collective-permute-done | bytes 1310752 | tf_op jit(solution)/shard_map/ppermute | solution.py:35
  46.3 0.4 collective-permute-start.14
  46.7 1.2 collective-permute-start.13
  47.9 4.1 %collective-permute-start.15 = (bf16[5,4,80,256]{3,2,1,0:T(8,128)(2,1)S(1)}, bf16[5,4,80,256]{3,2,1,0:T(8,128)(2,1)S(1)}, u32[]{:S(2)}, u32[]{:S(2)}) collective-permute-start(bf16[5,4,80,256]{3,2,1,0:T(8,128)(2,1)S(1)} %bitcast_dynamic-update-slice_fusion.5.mine), channel_id=1, source_target_pairs={{0,4},{4,0},{1,5},{5,1},{2,6},{6,2},{3,7},{7,3},{8,12},{12,8},{9,1... | collective-permute-start | bytes 2457608 | tf_op jit(solution)/shard_map/ppermute | solution.py:35
  52.0 5.4 %collective-permute-start.12 = (bf16[2,80,256]{2,1,0:T(8,128)(2,1)S(1)}, bf16[2,80,256]{2,1,0:T(8,128)(2,1)S(1)}, u32[]{:S(2)}, u32[]{:S(2)}) collective-permute-start(bf16[2,80,256]{2,1,0:T(8,128)(2,1)S(1)} %slice.19), channel_id=1, source_target_pairs={{0,56},{8,0},{16,8},{24,16},{32,24},{40,32},{48,40},{56,48},{1,57}... | collective-permute-start | bytes 245768 | tf_op jit(solution)/shard_map/ppermute | solution.py:35
  57.4 1.8 %collective-permute-done.12 = bf16[2,80,256]{2,1,0:T(8,128)(2,1)S(1)} collective-permute-done((bf16[2,80,256]{2,1,0:T(8,128)(2,1)S(1)}, bf16[2,80,256]{2,1,0:T(8,128)(2,1)S(1)}, u32[]{:S(2)}, u32[]{:S(2)}) %collective-permute-start.12) | collective-permute-done | bytes 81952 | tf_op jit(solution)/shard_map/ppermute | solution.py:35
  59.3 3.1 %collective-permute-done.11 = bf16[2,80,256]{2,1,0:T(8,128)(2,1)S(1)} collective-permute-done((bf16[2,80,256]{2,1,0:T(8,128)(2,1)S(1)}, bf16[2,80,256]{2,1,0:T(8,128)(2,1)S(1)}, u32[]{:S(2)}, u32[]{:S(2)}) %collective-permute-start.11) | collective-permute-done | bytes 81952 | tf_op jit(solution)/shard_map/ppermute | solution.py:35
  62.5 2.6 %collective-permute-start.16 = (bf16[3,4,80,256]{3,2,1,0:T(8,128)(2,1)S(1)}, bf16[3,4,80,256]{3,2,1,0:T(8,128)(2,1)S(1)}, u32[]{:S(2)}, u32[]{:S(2)}) collective-permute-start(bf16[3,4,80,256]{3,2,1,0:T(8,128)(2,1)S(1)} %pad_maximum_fusion.1.mine2), channel_id=1, source_target_pairs={{0,4},{4,0},{1,5},{5,1},{2,6},{6,2},{3,7},{7,3},{8,12},{12,8},{9,1... | collective-permute-start | bytes 1474568 | tf_op jit(solution)/shard_map/ppermute | solution.py:35
  65.0 2.7 %collective-permute-start.20 = (bf16[128,1024]{1,0:T(8,128)(2,1)S(1)}, bf16[128,1024]{1,0:T(8,128)(2,1)S(1)}, u32[]{:S(2)}, u32[]{:S(2)}) collective-permute-start(bf16[128,1024]{1,0:T(8,128)(2,1)S(1)} %copy-done.14), channel_id=1, source_target_pairs={{0,192},{64,0},{128,64},{192,128},{1,193},{65,1},{129,65},{193,129... | collective-permute-start | bytes 786440 | tf_op jit(solution)/shard_map/ppermute | solution.py:35
  67.8 4.1 %project_first.1 = (f32[3,2,128,128]{3,2,1,0:T(8,128)S(1)}, bf16[4,8,2,80,256]{4,3,2,1,0:T(8,128)(2,1)S(1)}) custom-call(s32[3]{0:T(128)S(1)} %copy-done.3, bf16[128,5120]{1,0:T(8,128)(2,1)S(1)} %copy-done, bf16[128,5120]{1,0:T(8,128)(2,1)S(1)} %collective-permute-done.9.left, bf16[128,5120]{1,0:T(8,128)(2,1)S(1)} %collective-permute-done.10.right, ...), custom_call_target="tpu_custom_call" | custom-call | tf_op jit(solution)/shard_map/project_first/pallas_call | solution.py:380
  71.9 0.7 project_last.1
  72.6 6.0 %collective-permute-start.18 = (bf16[512,256]{1,0:T(8,128)(2,1)S(1)}, bf16[512,256]{1,0:T(8,128)(2,1)S(1)}, u32[]{:S(2)}, u32[]{:S(2)}) collective-permute-start(bf16[512,256]{1,0:T(8,128)(2,1)S(1)} %project_last.1), channel_id=1, source_target_pairs={{0,56},{8,0},{16,8},{24,16},{32,24},{40,32},{48,40},{56,48},{1,57}... | collective-permute-start | bytes 786440 | tf_op jit(solution)/shard_map/ppermute | solution.py:35
  78.6 1.2 collective-permute-done.19.q1
  79.8 3.8 %collective-permute-done.18 = bf16[512,256]{1,0:T(8,128)(2,1)S(1)} collective-permute-done((bf16[512,256]{1,0:T(8,128)(2,1)S(1)}, bf16[512,256]{1,0:T(8,128)(2,1)S(1)}, u32[]{:S(2)}, u32[]{:S(2)}) %collective-permute-start.18) | collective-permute-done | bytes 262176 | tf_op jit(solution)/shard_map/ppermute | solution.py:35
  83.6 3.1 %collective-permute-done.17 = bf16[512,256]{1,0:T(8,128)(2,1)S(1)} collective-permute-done((bf16[512,256]{1,0:T(8,128)(2,1)S(1)}, bf16[512,256]{1,0:T(8,128)(2,1)S(1)}, u32[]{:S(2)}, u32[]{:S(2)}) %collective-permute-start.17) | collective-permute-done | bytes 262176 | tf_op jit(solution)/shard_map/ppermute | solution.py:35
  86.7 2.7 %collective-permute-start.23 = (bf16[512,256]{1,0:T(8,128)(2,1)S(1)}, bf16[512,256]{1,0:T(8,128)(2,1)S(1)}, u32[]{:S(2)}, u32[]{:S(2)}) collective-permute-start(bf16[512,256]{1,0:T(8,128)(2,1)S(1)} %collective-permute-done.18), channel_id=1, source_target_pairs={{0,56},{8,0},{16,8},{24,16},{32,24},{40,32},{48,40},{56,48},{1,57}... | collective-permute-start | bytes 786440 | tf_op jit(solution)/shard_map/ppermute | solution.py:35
  89.5 4.5 %collective-permute-done.22 = bf16[512,256]{1,0:T(8,128)(2,1)S(1)} collective-permute-done((bf16[512,256]{1,0:T(8,128)(2,1)S(1)}, bf16[512,256]{1,0:T(8,128)(2,1)S(1)}, u32[]{:S(2)}, u32[]{:S(2)}) %collective-permute-start.22) | collective-permute-done | bytes 262176 | tf_op jit(solution)/shard_map/ppermute | solution.py:35
  94.1 2.7 %collective-permute-start.28 = (bf16[5,512,256]{2,1,0:T(8,128)(2,1)S(1)}, bf16[5,512,256]{2,1,0:T(8,128)(2,1)S(1)}, u32[]{:S(2)}, u32[]{:S(2)}) collective-permute-start(bf16[5,512,256]{2,1,0:T(8,128)(2,1)S(1)} %bitcast_dynamic-update-slice_fusion.mine), channel_id=1, source_target_pairs={{0,4},{4,0},{1,5},{5,1},{2,6},{6,2},{3,7},{7,3},{8,12},{12,8},{9,1... | collective-permute-start | bytes 3932168 | tf_op jit(solution)/shard_map/ppermute | solution.py:35
  96.8 2.7 %collective-permute-start.25 = (bf16[512,256]{1,0:T(8,128)(2,1)S(1)}, bf16[512,256]{1,0:T(8,128)(2,1)S(1)}, u32[]{:S(2)}, u32[]{:S(2)}) collective-permute-start(bf16[512,256]{1,0:T(8,128)(2,1)S(1)} %collective-permute-done.23), channel_id=1, source_target_pairs={{0,56},{8,0},{16,8},{24,16},{32,24},{40,32},{48,40},{56,48},{1,57}... | collective-permute-start | bytes 786440 | tf_op jit(solution)/shard_map/ppermute | solution.py:35
  99.5 6.4 %collective-permute-done.24 = bf16[512,256]{1,0:T(8,128)(2,1)S(1)} collective-permute-done((bf16[512,256]{1,0:T(8,128)(2,1)S(1)}, bf16[512,256]{1,0:T(8,128)(2,1)S(1)}, u32[]{:S(2)}, u32[]{:S(2)}) %collective-permute-start.24) | collective-permute-done | bytes 262176 | tf_op jit(solution)/shard_map/ppermute | solution.py:35
  106.0 1.0 collective-permute-start.29
  106.9 0.3 collective-permute-start.26
  107.3 2.7 %collective-permute-start.27 = (bf16[256,256]{1,0:T(8,128)(2,1)S(1)}, bf16[256,256]{1,0:T(8,128)(2,1)S(1)}, u32[]{:S(2)}, u32[]{:S(2)}) collective-permute-start(bf16[256,256]{1,0:T(8,128)(2,1)S(1)} %slice.25), channel_id=1, source_target_pairs={{0,56},{8,0},{16,8},{24,16},{32,24},{40,32},{48,40},{56,48},{1,57}... | collective-permute-start | bytes 393224 | tf_op jit(solution)/shard_map/ppermute | solution.py:35
  110.0 3.5 %collective-permute-done.26 = bf16[256,256]{1,0:T(8,128)(2,1)S(1)} collective-permute-done((bf16[256,256]{1,0:T(8,128)(2,1)S(1)}, bf16[256,256]{1,0:T(8,128)(2,1)S(1)}, u32[]{:S(2)}, u32[]{:S(2)}) %collective-permute-start.26) | collective-permute-done | bytes 131104 | tf_op jit(solution)/shard_map/ppermute | solution.py:35
  113.6 0.9 collective-permute-start.30
  114.5 2.7 %prepare_queries.1.q_in = bf16[16,256,128]{2,1,0:T(8,128)(2,1)S(1)} custom-call(bf16[128,1024]{1,0:T(8,128)(2,1)S(1)} %copy-done.2, bf16[128,1024]{1,0:T(8,128)(2,1)S(1)} %collective-permute-done.19.q1, bf16[128,1024]{1,0:T(8,128)(2,1)S(1)} %collective-permute-done.20.q2, bf16[128,1024]{1,0:T(8,128)(2,1)S(1)} %collective-permute-done.21.q3, ...), custom_call_target="tpu_custom_call" | custom-call | tf_op jit(solution)/shard_map/prepare_queries/pallas_call | solution.py:406
  117.2 8.4 %attend.1 = (bf16[128,1024]{1,0:T(8,128)(2,1)S(1)}, bf16[128,1024]{1,0:T(8,128)(2,1)S(1)}, bf16[128,1024]{1,0:T(8,128)(2,1)S(1)}, bf16[128,1024]{1,0:T(8,128)(2,1)S(1)}) custom-call(s32[3]{0:T(128)S(1)} %copy-done.3, bf16[16,256,128]{2,1,0:T(8,128)(2,1)S(1)} %prepare_queries.1.q_in, bf16[5,512,256]{2,1,0:T(8,128)(2,1)S(1)} %bitcast_dynamic-update-slice_fusion.mine, ...), custom_call_target="tpu_custom_call" | custom-call | tf_op jit(solution)/shard_map/attend/pallas_call | solution.py:431
  125.6 0.7 copy-done.1
  126.3 1.0 collective-permute-start.31
  127.4 0.4 collective-permute-start.32
  127.8 2.6 %collective-permute-start.33 = (bf16[128,1024]{1,0:T(8,128)(2,1)S(1)}, bf16[128,1024]{1,0:T(8,128)(2,1)S(1)}, u32[]{:S(2)}, u32[]{:S(2)}) collective-permute-start(bf16[128,1024]{1,0:T(8,128)(2,1)S(1)} %get-tuple-element.106), channel_id=1, source_target_pairs={{0,128},{64,192},{128,0},{192,64},{1,129},{65,193},{129,1},{193,65... | collective-permute-start | bytes 786440 | tf_op jit(solution)/shard_map/ppermute | solution.py:35
  130.4 3.8 %collective-permute-done.31.refs_1_ = bf16[128,1024]{1,0:T(8,128)(2,1)S(1)} collective-permute-done((bf16[128,1024]{1,0:T(8,128)(2,1)S(1)}, bf16[128,1024]{1,0:T(8,128)(2,1)S(1)}, u32[]{:S(2)}, u32[]{:S(2)}) %collective-permute-start.31) | collective-permute-done | bytes 262176 | tf_op jit(solution)/shard_map/ppermute | solution.py:35
  134.2 1.9 %collective-permute-done.32.refs_2_ = bf16[128,1024]{1,0:T(8,128)(2,1)S(1)} collective-permute-done((bf16[128,1024]{1,0:T(8,128)(2,1)S(1)}, bf16[128,1024]{1,0:T(8,128)(2,1)S(1)}, u32[]{:S(2)}, u32[]{:S(2)}) %collective-permute-start.32) | collective-permute-done | bytes 262176 | tf_op jit(solution)/shard_map/ppermute | solution.py:35
  136.2 6.0 %collective-permute-done.33.refs_3_ = bf16[128,1024]{1,0:T(8,128)(2,1)S(1)} collective-permute-done((bf16[128,1024]{1,0:T(8,128)(2,1)S(1)}, bf16[128,1024]{1,0:T(8,128)(2,1)S(1)}, u32[]{:S(2)}, u32[]{:S(2)}) %collective-permute-start.33) | collective-permute-done | bytes 262176 | tf_op jit(solution)/shard_map/ppermute | solution.py:35
  142.2 0.7 copy-done.9
  142.9 2.2 %join_heads.1 = bf16[128,4096]{1,0:T(8,128)(2,1)} custom-call(s32[3]{0:T(128)} %pad_add_fusion.place, bf16[128,1024]{1,0:T(8,128)(2,1)} %copy-done.1, bf16[128,1024]{1,0:T(8,128)(2,1)} %copy-done.7, bf16[128,1024]{1,0:T(8,128)(2,1)} %copy-done.8, bf16[128,1024]{1,0:T(8,128)(2,1)} %copy-done.9), custom_call_target="tpu_custom_call" | custom-call | tf_op jit(solution)/shard_map/join_heads/pallas_call | solution.py:450
  (93 shorter events, 1.7 us)
Async XLA Ops:
  2.3 10.6 %collective-permute-start = (bf16[80,256]{1,0:T(8,128)(2,1)}, bf16[80,256]{1,0:T(8,128)(2,1)S(1)}, u32[]{:S(2)}, u32[]{:S(2)}) collective-permute-start(bf16[80,256]{1,0:T(8,128)(2,1)} %get-tuple-element.61), channel_id=1, source_target_pairs={{0,64},{64,128},{128,192},{192,0},{1,65},{65,129},{129,193},{193,1... | collective-permute-start | bytes 122888 | tf_op jit(solution)/shard_map/ppermute | solution.py:35
  4.3 8.6 %collective-permute-start.1 = (bf16[80,256]{1,0:T(8,128)(2,1)}, bf16[80,256]{1,0:T(8,128)(2,1)S(1)}, u32[]{:S(2)}, u32[]{:S(2)}) collective-permute-start(bf16[80,256]{1,0:T(8,128)(2,1)} %get-tuple-element.62), channel_id=1, source_target_pairs={{0,192},{64,0},{128,64},{192,128},{1,193},{65,1},{129,65},{193,129... | collective-permute-start | bytes 122888 | tf_op jit(solution)/shard_map/ppermute | solution.py:35
  5.7 7.3 %collective-permute-start.2 = (bf16[80,256]{1,0:T(8,128)(2,1)}, bf16[80,256]{1,0:T(8,128)(2,1)S(1)}, u32[]{:S(2)}, u32[]{:S(2)}) collective-permute-start(bf16[80,256]{1,0:T(8,128)(2,1)} %get-tuple-element.63), channel_id=1, source_target_pairs={{0,128},{64,192},{128,0},{192,64},{1,129},{65,193},{129,1},{193,65... | collective-permute-start | bytes 122888 | tf_op jit(solution)/shard_map/ppermute | solution.py:35
  12.9 0.6 copy-start.10
  12.9 0.6 copy-start.11
  13.6 0.6 copy-start.12
  15.7 29.0 %collective-permute-start.10 = (bf16[128,5120]{1,0:T(8,128)(2,1)}, bf16[128,5120]{1,0:T(8,128)(2,1)S(1)}, u32[]{:S(2)}, u32[]{:S(2)}) collective-permute-start(bf16[128,5120]{1,0:T(8,128)(2,1)} %norm_hidden.1.own), channel_id=1, source_target_pairs={{0,192},{64,0},{128,64},{192,128},{1,193},{65,1},{129,65},{193,129... | collective-permute-start | bytes 3932168 | tf_op jit(solution)/shard_map/ppermute | solution.py:35
  16.6 29.6 %collective-permute-start.9 = (bf16[128,5120]{1,0:T(8,128)(2,1)}, bf16[128,5120]{1,0:T(8,128)(2,1)S(1)}, u32[]{:S(2)}, u32[]{:S(2)}) collective-permute-start(bf16[128,5120]{1,0:T(8,128)(2,1)} %norm_hidden.1.own), channel_id=1, source_target_pairs={{0,64},{64,128},{128,192},{192,0},{1,65},{65,129},{129,193},{193,1... | collective-permute-start | bytes 3932168 | tf_op jit(solution)/shard_map/ppermute | solution.py:35
  19.9 1.3 copy-start.6
  21.2 7.9 %collective-permute-start.4 = (bf16[4,80,256]{2,1,0:T(8,128)(2,1)S(1)}, bf16[4,80,256]{2,1,0:T(8,128)(2,1)S(1)}, u32[]{:S(2)}, u32[]{:S(2)}) collective-permute-start(bf16[4,80,256]{2,1,0:T(8,128)(2,1)S(1)} %copy-done.6), channel_id=1, source_target_pairs={{0,56},{8,0},{16,8},{24,16},{32,24},{40,32},{48,40},{56,48},{1,57}... | collective-permute-start | bytes 491528 | tf_op jit(solution)/shard_map/ppermute | solution.py:35
  26.8 5.7 %collective-permute-start.3 = (bf16[4,80,256]{2,1,0:T(8,128)(2,1)S(1)}, bf16[4,80,256]{2,1,0:T(8,128)(2,1)S(1)}, u32[]{:S(2)}, u32[]{:S(2)}) collective-permute-start(bf16[4,80,256]{2,1,0:T(8,128)(2,1)S(1)} %copy-done.6), channel_id=1, source_target_pairs={{0,8},{8,16},{16,24},{24,32},{32,40},{40,48},{48,56},{56,0},{1,9},... | collective-permute-start | bytes 491528 | tf_op jit(solution)/shard_map/ppermute | solution.py:35
  32.8 5.8 %collective-permute-start.5 = (bf16[4,80,256]{2,1,0:T(8,128)(2,1)S(1)}, bf16[4,80,256]{2,1,0:T(8,128)(2,1)S(1)}, u32[]{:S(2)}, u32[]{:S(2)}) collective-permute-start(bf16[4,80,256]{2,1,0:T(8,128)(2,1)S(1)} %collective-permute-done.3), channel_id=1, source_target_pairs={{0,8},{8,16},{16,24},{24,32},{32,40},{40,48},{48,56},{56,0},{1,9},... | collective-permute-start | bytes 491528 | tf_op jit(solution)/shard_map/ppermute | solution.py:35
  32.9 5.7 %collective-permute-start.7 = (bf16[4,80,256]{2,1,0:T(8,128)(2,1)S(1)}, bf16[4,80,256]{2,1,0:T(8,128)(2,1)S(1)}, u32[]{:S(2)}, u32[]{:S(2)}) collective-permute-start(bf16[4,80,256]{2,1,0:T(8,128)(2,1)S(1)} %collective-permute-done.4), channel_id=1, source_target_pairs={{0,56},{8,0},{16,8},{24,16},{32,24},{40,32},{48,40},{56,48},{1,57}... | collective-permute-start | bytes 491528 | tf_op jit(solution)/shard_map/ppermute | solution.py:35
  38.5 5.7 %collective-permute-start.6 = (bf16[4,80,256]{2,1,0:T(8,128)(2,1)S(1)}, bf16[4,80,256]{2,1,0:T(8,128)(2,1)S(1)}, u32[]{:S(2)}, u32[]{:S(2)}) collective-permute-start(bf16[4,80,256]{2,1,0:T(8,128)(2,1)S(1)} %collective-permute-done.5), channel_id=1, source_target_pairs={{0,8},{8,16},{16,24},{24,32},{32,40},{40,48},{48,56},{56,0},{1,9},... | collective-permute-start | bytes 491528 | tf_op jit(solution)/shard_map/ppermute | solution.py:35
  38.5 5.7 %collective-permute-start.8 = (bf16[4,80,256]{2,1,0:T(8,128)(2,1)S(1)}, bf16[4,80,256]{2,1,0:T(8,128)(2,1)S(1)}, u32[]{:S(2)}, u32[]{:S(2)}) collective-permute-start(bf16[4,80,256]{2,1,0:T(8,128)(2,1)S(1)} %collective-permute-done.7), channel_id=1, source_target_pairs={{0,56},{8,0},{16,8},{24,16},{32,24},{40,32},{48,40},{56,48},{1,57}... | collective-permute-start | bytes 491528 | tf_op jit(solution)/shard_map/ppermute | solution.py:35
  46.2 18.8 %copy-start.15 = (bf16[128,1024]{1,0:T(8,128)(2,1)S(1)}, bf16[128,1024]{1,0:T(8,128)(2,1)}, u32[]{:S(2)}) copy-start(bf16[128,1024]{1,0:T(8,128)(2,1)} %get-tuple-element.91) | copy-start | bytes 786436
  46.3 18.8 %copy-start.14 = (bf16[128,1024]{1,0:T(8,128)(2,1)S(1)}, bf16[128,1024]{1,0:T(8,128)(2,1)}, u32[]{:S(2)}) copy-start(bf16[128,1024]{1,0:T(8,128)(2,1)} %get-tuple-element.92) | copy-start | bytes 786436
  46.3 21.4 %copy-start.13 = (bf16[128,1024]{1,0:T(8,128)(2,1)S(1)}, bf16[128,1024]{1,0:T(8,128)(2,1)}, u32[]{:S(2)}) copy-start(bf16[128,1024]{1,0:T(8,128)(2,1)} %get-tuple-element.93) | copy-start | bytes 786436
  46.3 21.5 %copy-start = (bf16[128,5120]{1,0:T(8,128)(2,1)S(1)}, bf16[128,5120]{1,0:T(8,128)(2,1)}, u32[]{:S(2)}) copy-start(bf16[128,5120]{1,0:T(8,128)(2,1)} %norm_hidden.1.own) | copy-start | bytes 3932164
  46.3 21.5 %copy-start.3 = (s32[3]{0:T(128)S(1)}, s32[3]{0:T(128)}, u32[]{:S(2)}) copy-start(s32[3]{0:T(128)} %pad_add_fusion.place) | copy-start | bytes 40
  46.3 21.5 %copy-start.4 = (f32[128]{0:T(128)S(1)}, f32[128]{0:T(128)}, u32[]{:S(2)}) copy-start(f32[128]{0:T(128)} %param.13) | copy-start | bytes 1540
  46.3 16.1 %collective-permute-start.14 = (bf16[64,5120]{1,0:T(8,128)(2,1)S(1)}, bf16[64,5120]{1,0:T(8,128)(2,1)S(1)}, u32[]{:S(2)}, u32[]{:S(2)}) collective-permute-start(bf16[64,5120]{1,0:T(8,128)(2,1)S(1)} %slice.21), channel_id=1, source_target_pairs={{0,192},{64,0},{128,64},{192,128},{1,193},{65,1},{129,65},{193,129... | collective-permute-start | bytes 1966088 | tf_op jit(solution)/shard_map/ppermute | solution.py:35
  46.7 15.8 %collective-permute-start.13 = (bf16[64,5120]{1,0:T(8,128)(2,1)S(1)}, bf16[64,5120]{1,0:T(8,128)(2,1)S(1)}, u32[]{:S(2)}, u32[]{:S(2)}) collective-permute-start(bf16[64,5120]{1,0:T(8,128)(2,1)S(1)} %slice.20), channel_id=1, source_target_pairs={{0,64},{64,128},{128,192},{192,0},{1,65},{65,129},{129,193},{193,1... | collective-permute-start | bytes 1966088 | tf_op jit(solution)/shard_map/ppermute | solution.py:35
  47.9 19.8 %collective-permute-start.15 = (bf16[5,4,80,256]{3,2,1,0:T(8,128)(2,1)S(1)}, bf16[5,4,80,256]{3,2,1,0:T(8,128)(2,1)S(1)}, u32[]{:S(2)}, u32[]{:S(2)}) collective-permute-start(bf16[5,4,80,256]{3,2,1,0:T(8,128)(2,1)S(1)} %bitcast_dynamic-update-slice_fusion.5.mine), channel_id=1, source_target_pairs={{0,4},{4,0},{1,5},{5,1},{2,6},{6,2},{3,7},{7,3},{8,12},{12,8},{9,1... | collective-permute-start | bytes 2457608 | tf_op jit(solution)/shard_map/ppermute | solution.py:35
  52.0 7.2 %collective-permute-start.12 = (bf16[2,80,256]{2,1,0:T(8,128)(2,1)S(1)}, bf16[2,80,256]{2,1,0:T(8,128)(2,1)S(1)}, u32[]{:S(2)}, u32[]{:S(2)}) collective-permute-start(bf16[2,80,256]{2,1,0:T(8,128)(2,1)S(1)} %slice.19), channel_id=1, source_target_pairs={{0,56},{8,0},{16,8},{24,16},{32,24},{40,32},{48,40},{56,48},{1,57}... | collective-permute-start | bytes 245768 | tf_op jit(solution)/shard_map/ppermute | solution.py:35
  57.4 4.9 %collective-permute-start.11 = (bf16[2,80,256]{2,1,0:T(8,128)(2,1)S(1)}, bf16[2,80,256]{2,1,0:T(8,128)(2,1)S(1)}, u32[]{:S(2)}, u32[]{:S(2)}) collective-permute-start(bf16[2,80,256]{2,1,0:T(8,128)(2,1)S(1)} %slice.18), channel_id=1, source_target_pairs={{0,8},{8,16},{16,24},{24,32},{32,40},{40,48},{48,56},{56,0},{1,9},... | collective-permute-start | bytes 245768 | tf_op jit(solution)/shard_map/ppermute | solution.py:35
  62.5 5.3 %collective-permute-start.16 = (bf16[3,4,80,256]{3,2,1,0:T(8,128)(2,1)S(1)}, bf16[3,4,80,256]{3,2,1,0:T(8,128)(2,1)S(1)}, u32[]{:S(2)}, u32[]{:S(2)}) collective-permute-start(bf16[3,4,80,256]{3,2,1,0:T(8,128)(2,1)S(1)} %pad_maximum_fusion.1.mine2), channel_id=1, source_target_pairs={{0,4},{4,0},{1,5},{5,1},{2,6},{6,2},{3,7},{7,3},{8,12},{12,8},{9,1... | collective-permute-start | bytes 1474568 | tf_op jit(solution)/shard_map/ppermute | solution.py:35
  65.0 14.8 %collective-permute-start.19 = (bf16[128,1024]{1,0:T(8,128)(2,1)S(1)}, bf16[128,1024]{1,0:T(8,128)(2,1)S(1)}, u32[]{:S(2)}, u32[]{:S(2)}) collective-permute-start(bf16[128,1024]{1,0:T(8,128)(2,1)S(1)} %copy-done.15), channel_id=1, source_target_pairs={{0,64},{64,128},{128,192},{192,0},{1,65},{65,129},{129,193},{193,1... | collective-permute-start | bytes 786440 | tf_op jit(solution)/shard_map/ppermute | solution.py:35
  65.0 14.8 %collective-permute-start.20 = (bf16[128,1024]{1,0:T(8,128)(2,1)S(1)}, bf16[128,1024]{1,0:T(8,128)(2,1)S(1)}, u32[]{:S(2)}, u32[]{:S(2)}) collective-permute-start(bf16[128,1024]{1,0:T(8,128)(2,1)S(1)} %copy-done.14), channel_id=1, source_target_pairs={{0,192},{64,0},{128,64},{192,128},{1,193},{65,1},{129,65},{193,129... | collective-permute-start | bytes 786440 | tf_op jit(solution)/shard_map/ppermute | solution.py:35
  67.7 12.1 %collective-permute-start.21 = (bf16[128,1024]{1,0:T(8,128)(2,1)S(1)}, bf16[128,1024]{1,0:T(8,128)(2,1)S(1)}, u32[]{:S(2)}, u32[]{:S(2)}) collective-permute-start(bf16[128,1024]{1,0:T(8,128)(2,1)S(1)} %copy-done.13), channel_id=1, source_target_pairs={{0,128},{64,192},{128,0},{192,64},{1,129},{65,193},{129,1},{193,65... | collective-permute-start | bytes 786440 | tf_op jit(solution)/shard_map/ppermute | solution.py:35
  72.6 11.1 %collective-permute-start.18 = (bf16[512,256]{1,0:T(8,128)(2,1)S(1)}, bf16[512,256]{1,0:T(8,128)(2,1)S(1)}, u32[]{:S(2)}, u32[]{:S(2)}) collective-permute-start(bf16[512,256]{1,0:T(8,128)(2,1)S(1)} %project_last.1), channel_id=1, source_target_pairs={{0,56},{8,0},{16,8},{24,16},{32,24},{40,32},{48,40},{56,48},{1,57}... | collective-permute-start | bytes 786440 | tf_op jit(solution)/shard_map/ppermute | solution.py:35
  78.5 8.2 %collective-permute-start.17 = (bf16[512,256]{1,0:T(8,128)(2,1)S(1)}, bf16[512,256]{1,0:T(8,128)(2,1)S(1)}, u32[]{:S(2)}, u32[]{:S(2)}) collective-permute-start(bf16[512,256]{1,0:T(8,128)(2,1)S(1)} %project_last.1), channel_id=1, source_target_pairs={{0,8},{8,16},{16,24},{24,32},{32,40},{40,48},{48,56},{56,0},{1,9},... | collective-permute-start | bytes 786440 | tf_op jit(solution)/shard_map/ppermute | solution.py:35
  86.7 7.3 %collective-permute-start.22 = (bf16[512,256]{1,0:T(8,128)(2,1)S(1)}, bf16[512,256]{1,0:T(8,128)(2,1)S(1)}, u32[]{:S(2)}, u32[]{:S(2)}) collective-permute-start(bf16[512,256]{1,0:T(8,128)(2,1)S(1)} %collective-permute-done.17), channel_id=1, source_target_pairs={{0,8},{8,16},{16,24},{24,32},{32,40},{40,48},{48,56},{56,0},{1,9},... | collective-permute-start | bytes 786440 | tf_op jit(solution)/shard_map/ppermute | solution.py:35
  86.7 7.3 %collective-permute-start.23 = (bf16[512,256]{1,0:T(8,128)(2,1)S(1)}, bf16[512,256]{1,0:T(8,128)(2,1)S(1)}, u32[]{:S(2)}, u32[]{:S(2)}) collective-permute-start(bf16[512,256]{1,0:T(8,128)(2,1)S(1)} %collective-permute-done.18), channel_id=1, source_target_pairs={{0,56},{8,0},{16,8},{24,16},{32,24},{40,32},{48,40},{56,48},{1,57}... | collective-permute-start | bytes 786440 | tf_op jit(solution)/shard_map/ppermute | solution.py:35
  94.0 20.5 %copy-start.2 = (bf16[128,1024]{1,0:T(8,128)(2,1)S(1)}, bf16[128,1024]{1,0:T(8,128)(2,1)}, u32[]{:S(2)}) copy-start(bf16[128,1024]{1,0:T(8,128)(2,1)} %get-tuple-element.94.q0) | copy-start | bytes 786436
  94.0 20.4 %copy-start.5 = (f32[128]{0:T(128)S(1)}, f32[128]{0:T(128)}, u32[]{:S(2)}) copy-start(f32[128]{0:T(128)} %param.12) | copy-start | bytes 1540
  94.1 23.1 %collective-permute-start.28 = (bf16[5,512,256]{2,1,0:T(8,128)(2,1)S(1)}, bf16[5,512,256]{2,1,0:T(8,128)(2,1)S(1)}, u32[]{:S(2)}, u32[]{:S(2)}) collective-permute-start(bf16[5,512,256]{2,1,0:T(8,128)(2,1)S(1)} %bitcast_dynamic-update-slice_fusion.mine), channel_id=1, source_target_pairs={{0,4},{4,0},{1,5},{5,1},{2,6},{6,2},{3,7},{7,3},{8,12},{12,8},{9,1... | collective-permute-start | bytes 3932168 | tf_op jit(solution)/shard_map/ppermute | solution.py:35
  96.8 9.1 %collective-permute-start.24 = (bf16[512,256]{1,0:T(8,128)(2,1)S(1)}, bf16[512,256]{1,0:T(8,128)(2,1)S(1)}, u32[]{:S(2)}, u32[]{:S(2)}) collective-permute-start(bf16[512,256]{1,0:T(8,128)(2,1)S(1)} %collective-permute-done.22), channel_id=1, source_target_pairs={{0,8},{8,16},{16,24},{24,32},{32,40},{40,48},{48,56},{56,0},{1,9},... | collective-permute-start | bytes 786440 | tf_op jit(solution)/shard_map/ppermute | solution.py:35
  96.8 9.1 %collective-permute-start.25 = (bf16[512,256]{1,0:T(8,128)(2,1)S(1)}, bf16[512,256]{1,0:T(8,128)(2,1)S(1)}, u32[]{:S(2)}, u32[]{:S(2)}) collective-permute-start(bf16[512,256]{1,0:T(8,128)(2,1)S(1)} %collective-permute-done.23), channel_id=1, source_target_pairs={{0,56},{8,0},{16,8},{24,16},{32,24},{40,32},{48,40},{56,48},{1,57}... | collective-permute-start | bytes 786440 | tf_op jit(solution)/shard_map/ppermute | solution.py:35
  106.0 11.2 %collective-permute-start.29 = (bf16[2,512,256]{2,1,0:T(8,128)(2,1)S(1)}, bf16[2,512,256]{2,1,0:T(8,128)(2,1)S(1)}, u32[]{:S(2)}, u32[]{:S(2)}) collective-permute-start(bf16[2,512,256]{2,1,0:T(8,128)(2,1)S(1)} %pad_maximum_fusion.mine2), channel_id=1, source_target_pairs={{0,4},{4,0},{1,5},{5,1},{2,6},{6,2},{3,7},{7,3},{8,12},{12,8},{9,1... | collective-permute-start | bytes 1572872 | tf_op jit(solution)/shard_map/ppermute | solution.py:35
  106.9 6.6 %collective-permute-start.26 = (bf16[256,256]{1,0:T(8,128)(2,1)S(1)}, bf16[256,256]{1,0:T(8,128)(2,1)S(1)}, u32[]{:S(2)}, u32[]{:S(2)}) collective-permute-start(bf16[256,256]{1,0:T(8,128)(2,1)S(1)} %slice.24), channel_id=1, source_target_pairs={{0,8},{8,16},{16,24},{24,32},{32,40},{40,48},{48,56},{56,0},{1,9},... | collective-permute-start | bytes 393224 | tf_op jit(solution)/shard_map/ppermute | solution.py:35
  107.3 6.3 %collective-permute-start.27 = (bf16[256,256]{1,0:T(8,128)(2,1)S(1)}, bf16[256,256]{1,0:T(8,128)(2,1)S(1)}, u32[]{:S(2)}, u32[]{:S(2)}) collective-permute-start(bf16[256,256]{1,0:T(8,128)(2,1)S(1)} %slice.25), channel_id=1, source_target_pairs={{0,56},{8,0},{16,8},{24,16},{32,24},{40,32},{48,40},{56,48},{1,57}... | collective-permute-start | bytes 393224 | tf_op jit(solution)/shard_map/ppermute | solution.py:35
  113.6 3.6 %collective-permute-start.30 = (bf16[1,512,256]{2,1,0:T(8,128)(2,1)S(1)}, bf16[1,512,256]{2,1,0:T(8,128)(2,1)S(1)}, u32[]{:S(2)}, u32[]{:S(2)}) collective-permute-start(bf16[1,512,256]{2,1,0:T(8,128)(2,1)S(1)} %maximum_bitcast_fusion.mine3), channel_id=1, source_target_pairs={{0,4},{4,0},{1,5},{5,1},{2,6},{6,2},{3,7},{7,3},{8,12},{12,8},{9,1... | collective-permute-start | bytes 786440 | tf_op jit(solution)/shard_map/ppermute | solution.py:35
  125.6 0.7 copy-start.1
  126.3 7.9 %collective-permute-start.31 = (bf16[128,1024]{1,0:T(8,128)(2,1)S(1)}, bf16[128,1024]{1,0:T(8,128)(2,1)S(1)}, u32[]{:S(2)}, u32[]{:S(2)}) collective-permute-start(bf16[128,1024]{1,0:T(8,128)(2,1)S(1)} %get-tuple-element.104), channel_id=1, source_target_pairs={{0,192},{64,0},{128,64},{192,128},{1,193},{65,1},{129,65},{193,129... | collective-permute-start | bytes 786440 | tf_op jit(solution)/shard_map/ppermute | solution.py:35
  127.4 8.8 %collective-permute-start.32 = (bf16[128,1024]{1,0:T(8,128)(2,1)S(1)}, bf16[128,1024]{1,0:T(8,128)(2,1)S(1)}, u32[]{:S(2)}, u32[]{:S(2)}) collective-permute-start(bf16[128,1024]{1,0:T(8,128)(2,1)S(1)} %get-tuple-element.105), channel_id=1, source_target_pairs={{0,64},{64,128},{128,192},{192,0},{1,65},{65,129},{129,193},{193,1... | collective-permute-start | bytes 786440 | tf_op jit(solution)/shard_map/ppermute | solution.py:35
  127.8 14.4 %collective-permute-start.33 = (bf16[128,1024]{1,0:T(8,128)(2,1)S(1)}, bf16[128,1024]{1,0:T(8,128)(2,1)S(1)}, u32[]{:S(2)}, u32[]{:S(2)}) collective-permute-start(bf16[128,1024]{1,0:T(8,128)(2,1)S(1)} %get-tuple-element.106), channel_id=1, source_target_pairs={{0,128},{64,192},{128,0},{192,64},{1,129},{65,193},{129,1},{193,65... | collective-permute-start | bytes 786440 | tf_op jit(solution)/shard_map/ppermute | solution.py:35
  134.2 7.9 %copy-start.7 = (bf16[128,1024]{1,0:T(8,128)(2,1)}, bf16[128,1024]{1,0:T(8,128)(2,1)S(1)}, u32[]{:S(2)}) copy-start(bf16[128,1024]{1,0:T(8,128)(2,1)S(1)} %collective-permute-done.31.refs_1_) | copy-start | bytes 786436
  136.2 6.0 %copy-start.8 = (bf16[128,1024]{1,0:T(8,128)(2,1)}, bf16[128,1024]{1,0:T(8,128)(2,1)S(1)}, u32[]{:S(2)}) copy-start(bf16[128,1024]{1,0:T(8,128)(2,1)S(1)} %collective-permute-done.32.refs_2_) | copy-start | bytes 786436
  142.2 0.7 copy-start.9
